TPU v7x, 256 devices: a whole 4x4x8 slice. The times are simulated.
256 devices in a mesh: gx: 64 (over y, z, core), gy: 4 (over x).
Axes of the slice: x: 4, y: 4, z: 8, core: 2. Of those that a mesh axis runs over, the one named last changes fastest.
Arguments:
- pressure: float32 [1024, 256, 256], P('gx', 'gy'), may hold values from -6 to 6
- previous: float32 [1024, 256, 256], P('gx', 'gy'), may hold values from -6 to 6
- oxygen_aux: float32 [1024, 256, 256], P('gx', 'gy'), may hold values from -3 to 3
- nitrogen_aux: float32 [1024, 256, 256], P('gx', 'gy'), may hold values from -3 to 3
- cell_class: int32 [1024, 256, 256], P('gx', 'gy'), may hold values from 0 to 7, as said below
- wall_admittance: float32 [8], replicated, may hold values from 0.1 to 1
- medium: float32 [5], replicated, may hold values from 0.3 to 0.9
Outputs:
- pressure_out: float32 [1024, 256, 256], P('gx', 'gy')
- previous_out: float32 [1024, 256, 256], P('gx', 'gy')
- oxygen_out: float32 [1024, 256, 256], P('gx', 'gy')
- nitrogen_out: float32 [1024, 256, 256], P('gx', 'gy')
Inputs may be any that keep to these rules, and one draw needn't show every extreme that they name: `cell_class`: class 0 is air; other classes index wall_admittance.
All inputs are finite; a program needn't handle non-finite values.
Results may differ from a plain program's by a relative error of at most 0.00002.
Values sent between devices are 32-bit elements; how exact they have to be, the bound alone decides.
A program may use at most 64 MiB of HBM per device.

v0:
```python
import jax
import jax.numpy as jnp
from jax import lax
from jax.sharding import PartitionSpec as P

STEPS = 4
NCLASS = 8


def extended(x, sides, width):
    for axis, dim in sides:
        devices, length = (lax.axis_size(axis), x.shape[dim])
        up = [(i, (i + 1) % devices) for i in range(devices - 1)]
        down = [(j, i) for i, j in up]
        last = lax.slice_in_dim(x, length - width, length, axis=dim)
        first = lax.slice_in_dim(x, 0, width, axis=dim)
        before = lax.ppermute(last, axis, up)
        after = lax.ppermute(first, axis, down)
        x = jnp.concatenate([before, x, after], axis=dim)
    return x


def laplace(field):
    center = field[1:-1, 1:-1]
    zpadded = jnp.pad(center, ((0, 0), (0, 0), (1, 1)))
    total = field[2:, 1:-1] + field[:-2, 1:-1]
    total = total + field[1:-1, 2:] + field[1:-1, :-2]
    total = total + zpadded[:, :, 2:] + zpadded[:, :, :-2]
    return total - 6.0 * center


def lookup(classes, wall_admittance):
    damping = jnp.zeros(classes.shape, jnp.float32)
    for number in range(1, NCLASS):
        damping = jnp.where(classes == number, wall_admittance[number], damping)
    return 0.5 * damping


def advance(padded, oxygen, nitrogen, boundary, medium):
    current = padded[0, 1:-1, 1:-1]
    earlier = padded[1, 1:-1, 1:-1]
    change = current - earlier
    oxygen = medium[0] * oxygen + medium[1] * change
    nitrogen = medium[2] * nitrogen + medium[3] * change
    update = 2.0 * current - (1.0 - boundary) * earlier + 0.33 * laplace(padded[0])
    update = update + 0.05 * medium[4] * laplace(padded[0] - padded[1]) - oxygen - nitrogen
    return (update / (1.0 + boundary), current, oxygen, nitrogen)


def per_device(pressure, previous, oxygen_aux, nitrogen_aux, cell_class, wall_admittance, medium):
    boundary = lookup(cell_class, wall_admittance)
    current, earlier, oxygen, nitrogen = (pressure, previous, oxygen_aux, nitrogen_aux)
    for step in range(STEPS):
        padded = extended(jnp.stack([current, earlier]), (("gx", 1), ("gy", 2)), 1)
        current, earlier, oxygen, nitrogen = advance(padded, oxygen, nitrogen, boundary, medium)
    return (current, earlier, oxygen, nitrogen)


def solution(mesh):
    return jax.shard_map(
        per_device,
        mesh=mesh,
        in_specs=(
            P("gx", "gy", None),
            P("gx", "gy", None),
            P("gx", "gy", None),
            P("gx", "gy", None),
            P("gx", "gy", None),
            P(),
            P(),
        ),
        out_specs=(
            P("gx", "gy", None),
            P("gx", "gy", None),
            P("gx", "gy", None),
            P("gx", "gy", None),
        ),
        check_vma=False,
    )
```

profile of v0, /device:TPU:26, one launch (start us, length us, event | category | flops | bytes accessed | tf_op | source)
XLA Modules:
  0.0 124.6 jit_solution(10454525216665692195)
XLA Ops:
  1.8 1.9 %collective-permute-start = (f32[2,1,64,256]{3,2,1,0:T(8,128)S(1)}, f32[2,1,64,256]{3,2,1,0:T(8,128)S(1)}, u32[]{:S(2)}, u32[]{:S(2)}) collective-permute-start(f32[2,1,64,256]{3,2,1,0:T(8,128)S(1)} %get-tuple-element.21), channel_id=1, source_target_pairs={{0,4},{4,8},{8,12},{12,16},{16,20},{20,24},{24,28},{28,32},{32,36}... | collective-permute-start | bytes 393224 | tf_op jit(solution)/shard_map/ppermute | solution.py:17
  3.7 7.4 %collective-permute-start.1 = (f32[2,1,64,256]{3,2,1,0:T(8,128)S(1)}, f32[2,1,64,256]{3,2,1,0:T(8,128)S(1)}, u32[]{:S(2)}, u32[]{:S(2)}) collective-permute-start(f32[2,1,64,256]{3,2,1,0:T(8,128)S(1)} %get-tuple-element.22), channel_id=1, source_target_pairs={{4,0},{8,4},{12,8},{16,12},{20,16},{24,20},{28,24},{32,28},{36,32}... | collective-permute-start | bytes 393224 | tf_op jit(solution)/shard_map/ppermute | solution.py:18
  13.6 3.4 %collective-permute-start.2 = (f32[2,18,1,256]{3,2,1,0:T(1,128)S(1)}, f32[2,18,1,256]{3,2,1,0:T(1,128)S(1)}, u32[]{:S(2)}, u32[]{:S(2)}) collective-permute-start(f32[2,18,1,256]{3,2,1,0:T(1,128)S(1)} %get-tuple-element.13), channel_id=1, source_target_pairs={{0,1},{1,2},{2,3},{4,5},{5,6},{6,7},{8,9},{9,10},{10,11},{12,13},{... | collective-permute-start | bytes 110600 | tf_op jit(solution)/shard_map/ppermute | solution.py:17
  17.1 2.4 %collective-permute-start.3 = (f32[2,18,1,256]{3,2,1,0:T(1,128)S(1)}, f32[2,18,1,256]{3,2,1,0:T(1,128)S(1)}, u32[]{:S(2)}, u32[]{:S(2)}) collective-permute-start(f32[2,18,1,256]{3,2,1,0:T(1,128)S(1)} %get-tuple-element.14), channel_id=1, source_target_pairs={{1,0},{2,1},{3,2},{5,4},{6,5},{7,6},{9,8},{10,9},{11,10},{13,12},{... | collective-permute-start | bytes 110600 | tf_op jit(solution)/shard_map/ppermute | solution.py:18
  20.8 2.1 %collective-permute-done.3 = f32[2,18,1,256]{3,2,1,0:T(1,128)S(1)} collective-permute-done((f32[2,18,1,256]{3,2,1,0:T(1,128)S(1)}, f32[2,18,1,256]{3,2,1,0:T(1,128)S(1)}, u32[]{:S(2)}, u32[]{:S(2)}) %collective-permute-start.3) | collective-permute-done | bytes 36896 | tf_op jit(solution)/shard_map/ppermute | solution.py:18
  25.4 9.8 %fusion.12 = f32[16,64,256]{2,1,0:T(8,128)S(1)} fusion(f32[16,64,256]{2,1,0:T(8,128)S(1)} %slice.392, f32[16,64,256]{2,1,0:T(8,128)S(1)} %slice.398, f32[18,66,256]{2,1,0:T(8,128)S(1)} %fusion.3, f32[18,66,256]{2,1,0:T(8,128)S(1)} %slice_bitcast_fusion.7, f32[16,64,256]{2,1,0:T(8,128)S(1)} %copy-done.1, f32[16,64,256]{2,1,0:T(8,128)S(1)} %copy-done, ...), kind=kLoop, calls=%fused_computation.40 | loop fusion | flops 12582912 | bytes 16777264 | tf_op jit(solution)/shard_map/div | solution.py:47
  35.3 1.9 %collective-permute-start.4 = (f32[2,1,64,256]{3,2,1,0:T(8,128)S(1)}, f32[2,1,64,256]{3,2,1,0:T(8,128)S(1)}, u32[]{:S(2)}, u32[]{:S(2)}) collective-permute-start(f32[2,1,64,256]{3,2,1,0:T(8,128)S(1)} %get-tuple-element.19), channel_id=1, source_target_pairs={{0,4},{4,8},{8,12},{12,16},{16,20},{20,24},{24,28},{28,32},{32,36}... | collective-permute-start | bytes 393224 | tf_op jit(solution)/shard_map/ppermute | solution.py:17
  37.2 5.8 %collective-permute-start.5 = (f32[2,1,64,256]{3,2,1,0:T(8,128)S(1)}, f32[2,1,64,256]{3,2,1,0:T(8,128)S(1)}, u32[]{:S(2)}, u32[]{:S(2)}) collective-permute-start(f32[2,1,64,256]{3,2,1,0:T(8,128)S(1)} %get-tuple-element.20), channel_id=1, source_target_pairs={{4,0},{8,4},{12,8},{16,12},{20,16},{24,20},{28,24},{32,28},{36,32}... | collective-permute-start | bytes 393224 | tf_op jit(solution)/shard_map/ppermute | solution.py:18
  45.5 3.1 %collective-permute-start.6 = (f32[2,18,1,256]{3,2,1,0:T(1,128)S(1)}, f32[2,18,1,256]{3,2,1,0:T(1,128)S(1)}, u32[]{:S(2)}, u32[]{:S(2)}) collective-permute-start(f32[2,18,1,256]{3,2,1,0:T(1,128)S(1)} %get-tuple-element.11), channel_id=1, source_target_pairs={{0,1},{1,2},{2,3},{4,5},{5,6},{6,7},{8,9},{9,10},{10,11},{12,13},{... | collective-permute-start | bytes 110600 | tf_op jit(solution)/shard_map/ppermute | solution.py:17
  48.6 2.7 %collective-permute-start.7 = (f32[2,18,1,256]{3,2,1,0:T(1,128)S(1)}, f32[2,18,1,256]{3,2,1,0:T(1,128)S(1)}, u32[]{:S(2)}, u32[]{:S(2)}) collective-permute-start(f32[2,18,1,256]{3,2,1,0:T(1,128)S(1)} %get-tuple-element.12), channel_id=1, source_target_pairs={{1,0},{2,1},{3,2},{5,4},{6,5},{7,6},{9,8},{10,9},{11,10},{13,12},{... | collective-permute-start | bytes 110600 | tf_op jit(solution)/shard_map/ppermute | solution.py:18
  51.4 3.1 %collective-permute-done.7 = f32[2,18,1,256]{3,2,1,0:T(1,128)S(1)} collective-permute-done((f32[2,18,1,256]{3,2,1,0:T(1,128)S(1)}, f32[2,18,1,256]{3,2,1,0:T(1,128)S(1)}, u32[]{:S(2)}, u32[]{:S(2)}) %collective-permute-start.7) | collective-permute-done | bytes 36896 | tf_op jit(solution)/shard_map/ppermute | solution.py:18
  55.3 10.0 %fusion.25 = f32[16,64,256]{2,1,0:T(8,128)S(1)} fusion(f32[16,64,256]{2,1,0:T(8,128)S(1)} %slice.404, f32[16,64,256]{2,1,0:T(8,128)S(1)} %slice.410, f32[18,66,256]{2,1,0:T(8,128)S(1)} %fusion.2, f32[18,66,256]{2,1,0:T(8,128)S(1)} %slice_bitcast_fusion.5, f32[16,64,256]{2,1,0:T(8,128)S(1)} %copy-done, f32[16,64,256]{2,1,0:T(8,128)S(1)} %fusion.12, ...), kind=kLoop, calls=%fused_computation.53 | loop fusion | flops 14417920 | bytes 17825840 | tf_op jit(solution)/shard_map/div | solution.py:47
  65.3 1.9 %collective-permute-start.8 = (f32[2,1,64,256]{3,2,1,0:T(8,128)S(1)}, f32[2,1,64,256]{3,2,1,0:T(8,128)S(1)}, u32[]{:S(2)}, u32[]{:S(2)}) collective-permute-start(f32[2,1,64,256]{3,2,1,0:T(8,128)S(1)} %get-tuple-element.17), channel_id=1, source_target_pairs={{0,4},{4,8},{8,12},{12,16},{16,20},{20,24},{24,28},{28,32},{32,36}... | collective-permute-start | bytes 393224 | tf_op jit(solution)/shard_map/ppermute | solution.py:17
  67.3 5.8 %collective-permute-start.9 = (f32[2,1,64,256]{3,2,1,0:T(8,128)S(1)}, f32[2,1,64,256]{3,2,1,0:T(8,128)S(1)}, u32[]{:S(2)}, u32[]{:S(2)}) collective-permute-start(f32[2,1,64,256]{3,2,1,0:T(8,128)S(1)} %get-tuple-element.18), channel_id=1, source_target_pairs={{4,0},{8,4},{12,8},{16,12},{20,16},{24,20},{28,24},{32,28},{36,32}... | collective-permute-start | bytes 393224 | tf_op jit(solution)/shard_map/ppermute | solution.py:18
  75.6 1.9 %collective-permute-start.10 = (f32[2,18,1,256]{3,2,1,0:T(1,128)S(1)}, f32[2,18,1,256]{3,2,1,0:T(1,128)S(1)}, u32[]{:S(2)}, u32[]{:S(2)}) collective-permute-start(f32[2,18,1,256]{3,2,1,0:T(1,128)S(1)} %get-tuple-element.9), channel_id=1, source_target_pairs={{0,1},{1,2},{2,3},{4,5},{5,6},{6,7},{8,9},{9,10},{10,11},{12,13},{... | collective-permute-start | bytes 110600 | tf_op jit(solution)/shard_map/ppermute | solution.py:17
  77.5 3.9 %collective-permute-start.11 = (f32[2,18,1,256]{3,2,1,0:T(1,128)S(1)}, f32[2,18,1,256]{3,2,1,0:T(1,128)S(1)}, u32[]{:S(2)}, u32[]{:S(2)}) collective-permute-start(f32[2,18,1,256]{3,2,1,0:T(1,128)S(1)} %get-tuple-element.10), channel_id=1, source_target_pairs={{1,0},{2,1},{3,2},{5,4},{6,5},{7,6},{9,8},{10,9},{11,10},{13,12},{... | collective-permute-start | bytes 110600 | tf_op jit(solution)/shard_map/ppermute | solution.py:18
  81.5 1.9 %collective-permute-done.11 = f32[2,18,1,256]{3,2,1,0:T(1,128)S(1)} collective-permute-done((f32[2,18,1,256]{3,2,1,0:T(1,128)S(1)}, f32[2,18,1,256]{3,2,1,0:T(1,128)S(1)}, u32[]{:S(2)}, u32[]{:S(2)}) %collective-permute-start.11) | collective-permute-done | bytes 36896 | tf_op jit(solution)/shard_map/ppermute | solution.py:18
  84.2 10.0 %fusion.38 = f32[16,64,256]{2,1,0:T(8,128)S(1)} fusion(f32[16,64,256]{2,1,0:T(8,128)S(1)} %slice.416, f32[16,64,256]{2,1,0:T(8,128)S(1)} %slice.422, f32[18,66,256]{2,1,0:T(8,128)S(1)} %fusion.1, f32[18,66,256]{2,1,0:T(8,128)S(1)} %slice_bitcast_fusion.3, f32[16,64,256]{2,1,0:T(8,128)S(1)} %fusion.12, f32[16,64,256]{2,1,0:T(8,128)S(1)} %fusion.25, ...), kind=kLoop, calls=%fused_computation.66 | loop fusion | flops 16252928 | bytes 18874416 | tf_op jit(solution)/shard_map/div | solution.py:47
  94.2 1.9 %collective-permute-start.12 = (f32[2,1,64,256]{3,2,1,0:T(8,128)S(1)}, f32[2,1,64,256]{3,2,1,0:T(8,128)S(1)}, u32[]{:S(2)}, u32[]{:S(2)}) collective-permute-start(f32[2,1,64,256]{3,2,1,0:T(8,128)S(1)} %get-tuple-element.15), channel_id=1, source_target_pairs={{0,4},{4,8},{8,12},{12,16},{16,20},{20,24},{24,28},{28,32},{32,36}... | collective-permute-start | bytes 393224 | tf_op jit(solution)/shard_map/ppermute | solution.py:17
  96.2 5.8 %collective-permute-start.13 = (f32[2,1,64,256]{3,2,1,0:T(8,128)S(1)}, f32[2,1,64,256]{3,2,1,0:T(8,128)S(1)}, u32[]{:S(2)}, u32[]{:S(2)}) collective-permute-start(f32[2,1,64,256]{3,2,1,0:T(8,128)S(1)} %get-tuple-element.16), channel_id=1, source_target_pairs={{4,0},{8,4},{12,8},{16,12},{20,16},{24,20},{28,24},{32,28},{36,32}... | collective-permute-start | bytes 393224 | tf_op jit(solution)/shard_map/ppermute | solution.py:18
  104.5 1.9 %collective-permute-start.14 = (f32[2,18,1,256]{3,2,1,0:T(1,128)S(1)}, f32[2,18,1,256]{3,2,1,0:T(1,128)S(1)}, u32[]{:S(2)}, u32[]{:S(2)}) collective-permute-start(f32[2,18,1,256]{3,2,1,0:T(1,128)S(1)} %get-tuple-element.7), channel_id=1, source_target_pairs={{0,1},{1,2},{2,3},{4,5},{5,6},{6,7},{8,9},{9,10},{10,11},{12,13},{... | collective-permute-start | bytes 110600 | tf_op jit(solution)/shard_map/ppermute | solution.py:17
  106.4 3.9 %collective-permute-start.15 = (f32[2,18,1,256]{3,2,1,0:T(1,128)S(1)}, f32[2,18,1,256]{3,2,1,0:T(1,128)S(1)}, u32[]{:S(2)}, u32[]{:S(2)}) collective-permute-start(f32[2,18,1,256]{3,2,1,0:T(1,128)S(1)} %get-tuple-element.8), channel_id=1, source_target_pairs={{1,0},{2,1},{3,2},{5,4},{6,5},{7,6},{9,8},{10,9},{11,10},{13,12},{... | collective-permute-start | bytes 110600 | tf_op jit(solution)/shard_map/ppermute | solution.py:18
  110.3 1.9 %collective-permute-done.15 = f32[2,18,1,256]{3,2,1,0:T(1,128)S(1)} collective-permute-done((f32[2,18,1,256]{3,2,1,0:T(1,128)S(1)}, f32[2,18,1,256]{3,2,1,0:T(1,128)S(1)}, u32[]{:S(2)}, u32[]{:S(2)}) %collective-permute-start.15) | collective-permute-done | bytes 36896 | tf_op jit(solution)/shard_map/ppermute | solution.py:18
  113.1 11.4 %fusion.51 = (f32[16,64,256]{2,1,0:T(8,128)}, f32[16,64,256]{2,1,0:T(8,128)}, f32[16,64,256]{2,1,0:T(8,128)}) fusion(f32[16,64,256]{2,1,0:T(8,128)S(1)} %slice.428, f32[16,64,256]{2,1,0:T(8,128)S(1)} %slice.434, f32[18,66,256]{2,1,0:T(8,128)S(1)} %fusion, f32[18,66,256]{2,1,0:T(8,128)S(1)} %slice_bitcast_fusion.1, f32[16,64,256]{2,1,0:T(8,128)S(1)} %fusion.25, ...), kind=kLoop, calls=%fused_computation.79 | loop fusion | flops 18087936 | bytes 22020144 | tf_op jit(solution)/shard_map/div | solution.py:47
  (56 shorter events, 16.9 us)
Async XLA Ops:
  0.6 13.0 %copy-start = (f32[16,64,256]{2,1,0:T(8,128)S(1)}, f32[16,64,256]{2,1,0:T(8,128)}, u32[]{:S(2)}) copy-start(f32[16,64,256]{2,1,0:T(8,128)} %param.7) | copy-start | bytes 3145732
  0.6 12.9 %copy-start.1 = (f32[16,64,256]{2,1,0:T(8,128)S(1)}, f32[16,64,256]{2,1,0:T(8,128)}, u32[]{:S(2)}) copy-start(f32[16,64,256]{2,1,0:T(8,128)} %param.8) | copy-start | bytes 3145732
  0.7 18.9 %copy-start.6 = (f32[5]{0:T(128)S(1)}, f32[5]{0:T(128)}, u32[]{:S(2)}) copy-start(f32[5]{0:T(128)} %param.13) | copy-start | bytes 64
  1.8 10.9 %collective-permute-start = (f32[2,1,64,256]{3,2,1,0:T(8,128)S(1)}, f32[2,1,64,256]{3,2,1,0:T(8,128)S(1)}, u32[]{:S(2)}, u32[]{:S(2)}) collective-permute-start(f32[2,1,64,256]{3,2,1,0:T(8,128)S(1)} %get-tuple-element.21), channel_id=1, source_target_pairs={{0,4},{4,8},{8,12},{12,16},{16,20},{20,24},{24,28},{28,32},{32,36}... | collective-permute-start | bytes 393224 | tf_op jit(solution)/shard_map/ppermute | solution.py:17
  3.7 9.9 %collective-permute-start.1 = (f32[2,1,64,256]{3,2,1,0:T(8,128)S(1)}, f32[2,1,64,256]{3,2,1,0:T(8,128)S(1)}, u32[]{:S(2)}, u32[]{:S(2)}) collective-permute-start(f32[2,1,64,256]{3,2,1,0:T(8,128)S(1)} %get-tuple-element.22), channel_id=1, source_target_pairs={{4,0},{8,4},{12,8},{16,12},{20,16},{24,20},{28,24},{32,28},{36,32}... | collective-permute-start | bytes 393224 | tf_op jit(solution)/shard_map/ppermute | solution.py:18
  13.6 7.2 %collective-permute-start.2 = (f32[2,18,1,256]{3,2,1,0:T(1,128)S(1)}, f32[2,18,1,256]{3,2,1,0:T(1,128)S(1)}, u32[]{:S(2)}, u32[]{:S(2)}) collective-permute-start(f32[2,18,1,256]{3,2,1,0:T(1,128)S(1)} %get-tuple-element.13), channel_id=1, source_target_pairs={{0,1},{1,2},{2,3},{4,5},{5,6},{6,7},{8,9},{9,10},{10,11},{12,13},{... | collective-permute-start | bytes 110600 | tf_op jit(solution)/shard_map/ppermute | solution.py:17
  17.1 5.9 %collective-permute-start.3 = (f32[2,18,1,256]{3,2,1,0:T(1,128)S(1)}, f32[2,18,1,256]{3,2,1,0:T(1,128)S(1)}, u32[]{:S(2)}, u32[]{:S(2)}) collective-permute-start(f32[2,18,1,256]{3,2,1,0:T(1,128)S(1)} %get-tuple-element.14), channel_id=1, source_target_pairs={{1,0},{2,1},{3,2},{5,4},{6,5},{7,6},{9,8},{10,9},{11,10},{13,12},{... | collective-permute-start | bytes 110600 | tf_op jit(solution)/shard_map/ppermute | solution.py:18
  23.5 1.2 copy-start.3
  23.5 1.5 %copy-start.4 = (f32[16,64,256]{2,1,0:T(8,128)S(1)}, f32[16,64,256]{2,1,0:T(8,128)}, u32[]{:S(2)}) copy-start(f32[16,64,256]{2,1,0:T(8,128)} %param.9) | copy-start | bytes 3145732
  23.5 1.8 %copy-start.5 = (s32[16,64,256]{2,1,0:T(8,128)S(1)}, s32[16,64,256]{2,1,0:T(8,128)}, u32[]{:S(2)}) copy-start(s32[16,64,256]{2,1,0:T(8,128)} %param.11) | copy-start | bytes 3145732
  35.3 8.4 %collective-permute-start.4 = (f32[2,1,64,256]{3,2,1,0:T(8,128)S(1)}, f32[2,1,64,256]{3,2,1,0:T(8,128)S(1)}, u32[]{:S(2)}, u32[]{:S(2)}) collective-permute-start(f32[2,1,64,256]{3,2,1,0:T(8,128)S(1)} %get-tuple-element.19), channel_id=1, source_target_pairs={{0,4},{4,8},{8,12},{12,16},{16,20},{20,24},{24,28},{28,32},{32,36}... | collective-permute-start | bytes 393224 | tf_op jit(solution)/shard_map/ppermute | solution.py:17
  37.2 8.3 %collective-permute-start.5 = (f32[2,1,64,256]{3,2,1,0:T(8,128)S(1)}, f32[2,1,64,256]{3,2,1,0:T(8,128)S(1)}, u32[]{:S(2)}, u32[]{:S(2)}) collective-permute-start(f32[2,1,64,256]{3,2,1,0:T(8,128)S(1)} %get-tuple-element.20), channel_id=1, source_target_pairs={{4,0},{8,4},{12,8},{16,12},{20,16},{24,20},{28,24},{32,28},{36,32}... | collective-permute-start | bytes 393224 | tf_op jit(solution)/shard_map/ppermute | solution.py:18
  45.5 5.9 %collective-permute-start.6 = (f32[2,18,1,256]{3,2,1,0:T(1,128)S(1)}, f32[2,18,1,256]{3,2,1,0:T(1,128)S(1)}, u32[]{:S(2)}, u32[]{:S(2)}) collective-permute-start(f32[2,18,1,256]{3,2,1,0:T(1,128)S(1)} %get-tuple-element.11), channel_id=1, source_target_pairs={{0,1},{1,2},{2,3},{4,5},{5,6},{6,7},{8,9},{9,10},{10,11},{12,13},{... | collective-permute-start | bytes 110600 | tf_op jit(solution)/shard_map/ppermute | solution.py:17
  48.6 5.9 %collective-permute-start.7 = (f32[2,18,1,256]{3,2,1,0:T(1,128)S(1)}, f32[2,18,1,256]{3,2,1,0:T(1,128)S(1)}, u32[]{:S(2)}, u32[]{:S(2)}) collective-permute-start(f32[2,18,1,256]{3,2,1,0:T(1,128)S(1)} %get-tuple-element.12), channel_id=1, source_target_pairs={{1,0},{2,1},{3,2},{5,4},{6,5},{7,6},{9,8},{10,9},{11,10},{13,12},{... | collective-permute-start | bytes 110600 | tf_op jit(solution)/shard_map/ppermute | solution.py:18
  65.3 8.4 %collective-permute-start.8 = (f32[2,1,64,256]{3,2,1,0:T(8,128)S(1)}, f32[2,1,64,256]{3,2,1,0:T(8,128)S(1)}, u32[]{:S(2)}, u32[]{:S(2)}) collective-permute-start(f32[2,1,64,256]{3,2,1,0:T(8,128)S(1)} %get-tuple-element.17), channel_id=1, source_target_pairs={{0,4},{4,8},{8,12},{12,16},{16,20},{20,24},{24,28},{28,32},{32,36}... | collective-permute-start | bytes 393224 | tf_op jit(solution)/shard_map/ppermute | solution.py:17
  67.3 8.3 %collective-permute-start.9 = (f32[2,1,64,256]{3,2,1,0:T(8,128)S(1)}, f32[2,1,64,256]{3,2,1,0:T(8,128)S(1)}, u32[]{:S(2)}, u32[]{:S(2)}) collective-permute-start(f32[2,1,64,256]{3,2,1,0:T(8,128)S(1)} %get-tuple-element.18), channel_id=1, source_target_pairs={{4,0},{8,4},{12,8},{16,12},{20,16},{24,20},{28,24},{32,28},{36,32}... | collective-permute-start | bytes 393224 | tf_op jit(solution)/shard_map/ppermute | solution.py:18
  75.6 5.9 %collective-permute-start.10 = (f32[2,18,1,256]{3,2,1,0:T(1,128)S(1)}, f32[2,18,1,256]{3,2,1,0:T(1,128)S(1)}, u32[]{:S(2)}, u32[]{:S(2)}) collective-permute-start(f32[2,18,1,256]{3,2,1,0:T(1,128)S(1)} %get-tuple-element.9), channel_id=1, source_target_pairs={{0,1},{1,2},{2,3},{4,5},{5,6},{6,7},{8,9},{9,10},{10,11},{12,13},{... | collective-permute-start | bytes 110600 | tf_op jit(solution)/shard_map/ppermute | solution.py:17
  77.5 5.9 %collective-permute-start.11 = (f32[2,18,1,256]{3,2,1,0:T(1,128)S(1)}, f32[2,18,1,256]{3,2,1,0:T(1,128)S(1)}, u32[]{:S(2)}, u32[]{:S(2)}) collective-permute-start(f32[2,18,1,256]{3,2,1,0:T(1,128)S(1)} %get-tuple-element.10), channel_id=1, source_target_pairs={{1,0},{2,1},{3,2},{5,4},{6,5},{7,6},{9,8},{10,9},{11,10},{13,12},{... | collective-permute-start | bytes 110600 | tf_op jit(solution)/shard_map/ppermute | solution.py:18
  94.2 18.9 %copy-start.2 = (f32[16,64,256]{2,1,0:T(8,128)}, f32[16,64,256]{2,1,0:T(8,128)S(1)}, u32[]{:S(2)}) copy-start(f32[16,64,256]{2,1,0:T(8,128)S(1)} %fusion.38) | copy-start | bytes 3145732
  94.2 8.4 %collective-permute-start.12 = (f32[2,1,64,256]{3,2,1,0:T(8,128)S(1)}, f32[2,1,64,256]{3,2,1,0:T(8,128)S(1)}, u32[]{:S(2)}, u32[]{:S(2)}) collective-permute-start(f32[2,1,64,256]{3,2,1,0:T(8,128)S(1)} %get-tuple-element.15), channel_id=1, source_target_pairs={{0,4},{4,8},{8,12},{12,16},{16,20},{20,24},{24,28},{28,32},{32,36}... | collective-permute-start | bytes 393224 | tf_op jit(solution)/shard_map/ppermute | solution.py:17
  96.2 8.3 %collective-permute-start.13 = (f32[2,1,64,256]{3,2,1,0:T(8,128)S(1)}, f32[2,1,64,256]{3,2,1,0:T(8,128)S(1)}, u32[]{:S(2)}, u32[]{:S(2)}) collective-permute-start(f32[2,1,64,256]{3,2,1,0:T(8,128)S(1)} %get-tuple-element.16), channel_id=1, source_target_pairs={{4,0},{8,4},{12,8},{16,12},{20,16},{24,20},{28,24},{32,28},{36,32}... | collective-permute-start | bytes 393224 | tf_op jit(solution)/shard_map/ppermute | solution.py:18
  104.5 5.9 %collective-permute-start.14 = (f32[2,18,1,256]{3,2,1,0:T(1,128)S(1)}, f32[2,18,1,256]{3,2,1,0:T(1,128)S(1)}, u32[]{:S(2)}, u32[]{:S(2)}) collective-permute-start(f32[2,18,1,256]{3,2,1,0:T(1,128)S(1)} %get-tuple-element.7), channel_id=1, source_target_pairs={{0,1},{1,2},{2,3},{4,5},{5,6},{6,7},{8,9},{9,10},{10,11},{12,13},{... | collective-permute-start | bytes 110600 | tf_op jit(solution)/shard_map/ppermute | solution.py:17
  106.4 5.9 %collective-permute-start.15 = (f32[2,18,1,256]{3,2,1,0:T(1,128)S(1)}, f32[2,18,1,256]{3,2,1,0:T(1,128)S(1)}, u32[]{:S(2)}, u32[]{:S(2)}) collective-permute-start(f32[2,18,1,256]{3,2,1,0:T(1,128)S(1)} %get-tuple-element.8), channel_id=1, source_target_pairs={{1,0},{2,1},{3,2},{5,4},{6,5},{7,6},{9,8},{10,9},{11,10},{13,12},{... | collective-permute-start | bytes 110600 | tf_op jit(solution)/shard_map/ppermute | solution.py:18
where the time goes:
time: 127 us; the launch traced here: 125 us
  starting transfers between devices  55.7 us (44%)
  other arithmetic  44.6 us (35%)
  waiting for transfers between devices  17.4 us (14%)
  local copies, waits for them, and re-layouts  5.07 us (4%)
  between operations  1.74 us (1%)
    div x4, other arithmetic, advance(): return (update / (1.0 + boundary), current, oxygen, nitrogen)  41.2 us
    ppermute x8, starting transfers between devices, extended(): after = lax.ppermute(first, axis, down)  37.7 us
    ppermute x8, starting transfers between devices, extended(): before = lax.ppermute(last, axis, up)  18 us
    ppermute x8, waiting for transfers between devices, extended(): after = lax.ppermute(first, axis, down)  15.3 us
  transfers between devices with their start and end apart: 16, of which 11 were waited for; matrix products, arithmetic and copies ran while one was open for 2% of the time, Pallas kernels for 0%

commit v1 on v0

v1 whole, which is shorter than its diff:
```python
import functools

import jax
import jax.numpy as jnp
from jax import lax
from jax.experimental import pallas as pl
from jax.experimental.pallas import tpu as pltpu
from jax.sharding import PartitionSpec as P

STEPS = 4
NCLASS = 8
MESH = pl.DeviceIdType.MESH
LANES = 128
PAD = 8


def steps_kernel(nx, ny, p_hbm, q_hbm, o_hbm, n_hbm, c_hbm, wall, medium, A, B, O, N,
                 cls, adm, even, odd, gs, ys, yg, cs, xr, yr, yrg, cr,
                 load_sem, send_sem, recv_sem):
    X, H, Y, _ = A.shape
    T = Y // 8
    gx, gy = lax.axis_index("gx"), lax.axis_index("gy")
    xs = (lax.rem(gx + nx - 1, nx), lax.rem(gx + 1, nx))
    yside = (lax.rem(gy + ny - 1, ny), lax.rem(gy + 1, ny))
    barrier = pltpu.get_barrier_semaphore()
    others = [(xs[0], gy), (xs[1], gy), (gx, yside[0]), (gx, yside[1])]
    others += [(xs[i], yside[j]) for i in range(2) for j in range(2)]
    for other in others:
        pl.semaphore_signal(barrier, inc=1, device_id=other, device_id_type=MESH)

    loads = {}
    for at, (name, src, dst) in enumerate(
        (("p", p_hbm, A), ("q", q_hbm, B), ("c", c_hbm, cls), ("o", o_hbm, O), ("n", n_hbm, N))
    ):
        loads[name] = [
            pltpu.make_async_copy(src.at[:, :, pl.ds(LANES * h, LANES)], dst.at[:, h], load_sem.at[at, h])
            for h in range(H)
        ]
        for copy in loads[name]:
            copy.start()

    m0, m1, m2, m3 = medium[0], medium[1], medium[2], medium[3]
    c = 0.05 * medium[4]
    al = 0.33 + c
    inside = [gx > 0, gx < nx - 1]
    mx = [jnp.where(inside[s], 1.0, 0.0).astype(jnp.float32) for s in range(2)]
    my = [jnp.where(t, 1.0, 0.0).astype(jnp.float32) for t in (gy > 0, gy < ny - 1)]

    lane = lax.broadcasted_iota(jnp.int32, (8, LANES), 1)
    first, last = lane == 0, lane == LANES - 1
    zero = jnp.zeros((8, LANES), jnp.float32)

    def rows(j):
        return pl.ds(8 * j, 8)

    def wrows(j, by=0):
        return pl.ds(PAD + 8 * j + by, 8)

    def edge_rows(s):
        return 0 if s == 0 else Y - 1

    def tile(x, j, now, then, src, dst, keep=None):
        w = [src[x + 1, h, wrows(j), :] for h in range(H)]
        down = [pltpu.roll(v, 1, 1) for v in w]
        up = [pltpu.roll(v, LANES - 1, 1) for v in w]
        below = [jnp.where(first, 0.0, down[0]), jnp.where(first, down[0], down[1])]
        above = [jnp.where(last, up[1], up[0]), jnp.where(last, 0.0, up[1])]
        for h in range(H):
            p, q = now[x, h, rows(j), :], then[x, h, rows(j), :]
            total = src[x, h, wrows(j), :] + src[x + 2, h, wrows(j), :]
            total = total + (src[x + 1, h, wrows(j, -1), :] + src[x + 1, h, wrows(j, 1), :])
            total = total + (below[h] + above[h])
            d = p - q
            o = m0 * O[x, h, rows(j), :] + m1 * d
            n = m2 * N[x, h, rows(j), :] + m3 * d
            new = q + adm[x, h, rows(j), :] * ((total - 6.0 * w[h]) + (2.0 * d - (o + n)))
            v = al * new - c * p
            then[x, h, rows(j), :] = new
            O[x, h, rows(j), :] = o
            N[x, h, rows(j), :] = n
            dst[x + 1, h, wrows(j), :] = v
            if keep is not None:
                gs[keep, h, rows(j), :] = v

    def loop(count, body, unroll=1):
        lax.fori_loop(0, count, lambda i, carry: (body(i), carry)[1], 0, unroll=unroll)

    flat_even = even.reshape((X + 2) * H * (Y + 2 * PAD), LANES)
    flat_odd = odd.reshape((X + 2) * H * (Y + 2 * PAD), LANES)
    flat_a = adm.reshape(X * H * Y, LANES)
    flat_b = B.reshape(X * H * Y, LANES)

    def wline(h, y):
        step = H * (Y + 2 * PAD)
        return pl.ds(step + h * (Y + 2 * PAD) + PAD + y, X, stride=step)

    def line(h, y):
        return pl.ds(h * Y + y, X, stride=H * Y)

    def send(at, src, dst, device):
        copy = pltpu.make_async_remote_copy(
            src_ref=src, dst_ref=dst, send_sem=send_sem.at[at], recv_sem=recv_sem.at[at],
            device_id=device, device_id_type=MESH)
        copy.start()
        return copy

    def clear(x):
        for h in range(H):
            even[x, h, pl.ds(0, PAD), :] = zero
            even[x, h, pl.ds(PAD + Y, PAD), :] = zero

    loop(X + 2, clear)

    def clear_planes(j):
        for x in (0, X + 1):
            for h in range(H):
                even[x, h, wrows(j), :] = zero

    loop(T, clear_planes)

    for name in ("p", "q"):
        for copy in loads[name]:
            copy.wait()

    def first_w(x):
        for j in range(T):
            for h in range(H):
                even[x + 1, h, wrows(j), :] = al * A[x, h, rows(j), :] - c * B[x, h, rows(j), :]

    loop(X, first_w)

    table = [1.0 / (1.0 + 0.5 * jnp.full((8, LANES), wall[k], jnp.float32)) for k in range(1, NCLASS)]
    for copy in loads["c"]:
        copy.wait()

    def admit(x):
        for j in range(T):
            for h in range(H):
                kind = cls[x, h, rows(j), :]
                a = jnp.ones((8, LANES), jnp.float32)
                for k in range(1, NCLASS):
                    a = jnp.where(kind == k, table[k - 1], a)
                adm[x, h, rows(j), :] = a

    loop(X, admit)

    pending = {}
    message = iter(range(64))
    pl.semaphore_wait(barrier, len(others))

    def send_planes(e):
        for s in range(2):
            pending["w", e, s] = send(
                next(message), even.at[1 if s == 0 else X, :, pl.ds(PAD, Y), :], xr.at[e, 0, 1 - s], (xs[s], gy))

    def send_corners(e):
        for s in range(2):
            for t in range(2):
                for h in range(H):
                    cs[e, s, t, pl.ds(h, 1), :] = even[1 if s == 0 else X, h, pl.ds(PAD + edge_rows(t), 1), :]
                pending["c", e, s, t] = send(
                    next(message), cs.at[e, s, t], cr.at[e, 1 - s, 1 - t], (xs[s], yside[t]))

    def send_lines(e):
        for t in range(2):
            for h in range(H):
                ys[e, t, 0, h] = flat_even[wline(h, edge_rows(t)), :]
                if e == 0:
                    ys[e, t, 1, h] = flat_a[line(h, edge_rows(t)), :]
            fields = 2 if e == 0 else 1
            pending["y", e, t] = send(
                next(message), ys.at[e, t, pl.ds(0, fields)], yr.at[e, 1 - t, pl.ds(0, fields)], (gx, yside[t]))

    for e in range(STEPS // 2):
        if e == 0:
            send_planes(e)
            send_lines(e)
            send_corners(e)
            for s in range(2):
                pending["a", s] = send(
                    next(message), adm.at[0 if s == 0 else X - 1], xr.at[0, 2, 1 - s], (xs[s], gy))
            for name in ("o", "n"):
                for copy in loads[name]:
                    copy.wait()

        def first_planes(i, e=e):
            for j in range(T):
                tile((X - 1) * i, j, A, B, even, odd, keep=2 * e + i)

        loop(2, first_planes)
        for s in range(2):
            pending["g", e, s] = send(next(message), gs.at[2 * e + s], xr.at[e, 1, 1 - s], (xs[s], gy))

        if e > 0:
            def rest(i):
                for j in (0, T - 1):
                    tile(i + 2, j, B, A, odd, even)

            loop(X - 4, rest, 2)
            send_lines(e)

        def plane(i):
            for j in range(T):
                tile(i + 1, j, A, B, even, odd)

        loop(X - 2, plane, 2)
        for t in range(2):
            for h in range(H):
                yg[e, t, h] = flat_odd[wline(h, edge_rows(t)), :]
            pending["yg", e, t] = send(next(message), yg.at[e, t], yrg.at[e, 1 - t], (gx, yside[t]))

        def inner(i):
            for j in range(1, T - 1):
                tile(i + 2, j, B, A, odd, even)

        loop(X - 4, inner, 2)

        for t in range(2):
            pending["y", e, t].wait_recv()
        for t in range(2):
            for h in range(H):
                add = flat_a[line(h, edge_rows(t)), :] * (my[t] * yr[e, t, 0, h])
                flat_b[line(h, edge_rows(t)), :] = flat_b[line(h, edge_rows(t)), :] + add
                flat_odd[wline(h, edge_rows(t)), :] = flat_odd[wline(h, edge_rows(t)), :] + al * add
        for t in range(2):
            pending["yg", e, t].wait_recv()
        for t in range(2):
            for h in range(H):
                y = -1 if t == 0 else Y
                flat_odd[wline(h, y), :] = my[t] * (yrg[e, t, h] + al * yr[0, t, 1, h] * ys[e, t, 0, h])
        for s in range(2):
            pending["w", e, s].wait_recv()
        for s in range(2):
            x = 0 if s == 0 else X - 1

            def face(j, s=s, x=x, e=e):
                for h in range(H):
                    add = adm[x, h, rows(j), :] * (mx[s] * xr[e, 0, s, h, rows(j), :])
                    B[x, h, rows(j), :] = B[x, h, rows(j), :] + add
                    odd[x + 1, h, wrows(j), :] = odd[x + 1, h, wrows(j), :] + al * add

            loop(T, face, T)
        for s in range(2):
            if e == 0:
                pending["a", s].wait_recv()
            pending["g", e, s].wait_recv()
        for s in range(2):
            x, halo = (0, 0) if s == 0 else (X - 1, X + 1)

            def layer(j, s=s, x=x, halo=halo, e=e):
                for h in range(H):
                    odd[halo, h, wrows(j), :] = mx[s] * (
                        xr[e, 1, s, h, rows(j), :]
                        + al * xr[0, 2, s, h, rows(j), :] * even[x + 1, h, wrows(j), :])

            loop(T, layer, T)
        for s in range(2):
            for t in range(2):
                pending["c", e, s, t].wait_recv()
        for s in range(2):
            x, halo = (1, 0) if s == 0 else (X, X + 1)
            for t in range(2):
                y, over = (0, -1) if t == 0 else (Y - 1, Y)
                for h in range(H):
                    scaled = (mx[s] * my[t] * al) * cr[e, s, t, pl.ds(h, 1), :]
                    at = pl.ds(PAD + y, 1)
                    odd[halo, h, at, :] = odd[halo, h, at, :] + xr[0, 2, s, h, pl.ds(y, 1), :] * scaled
                    at = pl.ds(PAD + over, 1)
                    odd[x, h, at, :] = odd[x, h, at, :] + yr[0, t, 1, h, pl.ds(x - 1, 1), :] * scaled
            pending["w", e, s].wait_send()

        def ends(i):
            for j in range(T):
                tile((X - 1) * i, j, B, A, odd, even)

        loop(2, ends)
        if e == 0:
            send_planes(1)
            send_corners(1)

        def next_ends(i):
            for j in range(T):
                tile(1 + (X - 3) * i, j, B, A, odd, even)

        loop(2, next_ends)
        if e > 0:
            def rest_last(i):
                for j in (0, T - 1):
                    tile(i + 2, j, B, A, odd, even)

            loop(X - 4, rest_last, 2)

    for name, copy in pending.items():
        if name[0] != "w":
            copy.wait_send()


def store_kernel(a, b, o, n, p_out, q_out, o_out, n_out, sems):
    copies = [
        pltpu.make_async_copy(src.at[:, h], dst.at[:, :, pl.ds(LANES * h, LANES)], sems.at[at, h])
        for at, (src, dst) in enumerate(((a, p_out), (b, q_out), (o, o_out), (n, n_out)))
        for h in range(2)
    ]
    for copy in copies:
        copy.start()
    for copy in copies:
        copy.wait()


def per_device(nx, ny, pressure, previous, oxygen_aux, nitrogen_aux, cell_class, wall_admittance, medium):
    X, Y, Z = pressure.shape
    H = Z // LANES
    split = (X, H, Y, LANES)
    padded = (X + 2, H, Y + 2 * PAD, LANES)
    hbm = pl.BlockSpec(memory_space=pl.ANY)
    vmem = pl.BlockSpec(memory_space=pltpu.VMEM)
    smem = pl.BlockSpec(memory_space=pltpu.SMEM)
    f32 = jnp.float32
    state = pl.pallas_call(
        functools.partial(steps_kernel, nx, ny),
        out_shape=[pltpu.VMEM(split, f32)] * 4,
        in_specs=[hbm] * 5 + [smem] * 2,
        out_specs=[vmem] * 4,
        scratch_shapes=[
            pltpu.VMEM(split, jnp.int32),
            pltpu.VMEM(split, f32),
            pltpu.VMEM(padded, f32),
            pltpu.VMEM(padded, f32),
            pltpu.VMEM((4, H, Y, LANES), f32),
            pltpu.VMEM((2, 2, 2, H, X, LANES), f32),
            pltpu.VMEM((2, 2, H, X, LANES), f32),
            pltpu.VMEM((2, 2, 2, 8, LANES), f32),
            pltpu.VMEM((2, 3, 2, H, Y, LANES), f32),
            pltpu.VMEM((2, 2, 2, H, X, LANES), f32),
            pltpu.VMEM((2, 2, H, X, LANES), f32),
            pltpu.VMEM((2, 2, 2, 8, LANES), f32),
            pltpu.SemaphoreType.DMA((5, 2)),
            pltpu.SemaphoreType.DMA((32,)),
            pltpu.SemaphoreType.DMA((32,)),
        ],
        compiler_params=pltpu.CompilerParams(
            collective_id=0, has_side_effects=True, vmem_limit_bytes=56 << 20),
    )(pressure, previous, oxygen_aux, nitrogen_aux, cell_class, wall_admittance, medium)
    out = pl.pallas_call(
        store_kernel,
        out_shape=[jax.ShapeDtypeStruct((X, Y, Z), f32)] * 4,
        in_specs=[vmem] * 4,
        out_specs=[hbm] * 4,
        scratch_shapes=[pltpu.SemaphoreType.DMA((4, 2))],
        compiler_params=pltpu.CompilerParams(vmem_limit_bytes=16 << 20),
    )(*state)
    return tuple(out)


def solution(mesh):
    field = P("gx", "gy", None)
    return jax.shard_map(
        functools.partial(per_device, mesh.shape["gx"], mesh.shape["gy"]),
        mesh=mesh,
        in_specs=(field,) * 5 + (P(), P()),
        out_specs=(field,) * 4,
        check_vma=False,
    )
```

time: 127 us -> 26.2 us (0.21)
  the two profiles are of different devices: /device:TPU:26 before, /device:TPU:2 now
where the time goes in v1:
time: 26.2 us; the launch traced here: 26.1 us
  Pallas kernels  25.4 us (97%)
  between operations  0.64 us (2%)
    pallas_call x1, Pallas kernels, per_device(): pl.pallas_call(functools.partial(steps_kernel, nx, ny), out_shape=[pltpu....  23.4 us
    pallas_call x1, Pallas kernels, per_device(): pl.pallas_call(store_kernel, out_shape=[jax.ShapeDtypeStruct((X, Y, Z), f...  2.07 us

profile of v1, /device:TPU:2, one launch (start us, length us, event | category | flops | bytes accessed | tf_op | source)
XLA Modules:
  0.0 26.1 jit_solution(8414484720331405109)
XLA Ops:
  0.6 23.4 %shard_map.102 = (f32[16,2,64,128]{3,2,1,0:T(8,128)S(1)}, f32[16,2,64,128]{3,2,1,0:T(8,128)S(1)}, f32[16,2,64,128]{3,2,1,0:T(8,128)S(1)}, f32[16,2,64,128]{3,2,1,0:T(8,128)S(1)}) custom-call(f32[16,64,256]{2,1,0:T(8,128)} %p_hbm.1, f32[16,64,256]{2,1,0:T(8,128)} %q_hbm.1, f32[16,64,256]{2,1,0:T(8,128)} %o_hbm.1, f32[16,64,256]{2,1,0:T(8,128)} %n_hbm.1, ...), custom_call_target="tpu_custom_call" | custom-call | tf_op jit(solution)/shard_map/pallas_call | solution.py:319
  24.0 2.1 %shard_map.103 = (f32[16,64,256]{2,1,0:T(8,128)}, f32[16,64,256]{2,1,0:T(8,128)}, f32[16,64,256]{2,1,0:T(8,128)}, f32[16,64,256]{2,1,0:T(8,128)}) custom-call(f32[16,2,64,128]{3,2,1,0:T(8,128)S(1)} %get-tuple-element.8.a, f32[16,2,64,128]{3,2,1,0:T(8,128)S(1)} %get-tuple-element.9.b, f32[16,2,64,128]{3,2,1,0:T(8,128)S(1)} %get-tuple-element.10.o, ...), custom_call_target="tpu_custom_call" | custom-call | tf_op jit(solution)/shard_map/pallas_call | solution.py:344

commit v2 on v1

--- a/solution.py
+++ b/solution.py
@@ -25,8 +25,14 @@
     barrier = pltpu.get_barrier_semaphore()
     others = [(xs[0], gy), (xs[1], gy), (gx, yside[0]), (gx, yside[1])]
     others += [(xs[i], yside[j]) for i in range(2) for j in range(2)]
-    for other in others:
-        pl.semaphore_signal(barrier, inc=1, device_id=other, device_id_type=MESH)
+    there_x = (gx > 0, gx < nx - 1)
+    there_y = (gy > 0, gy < ny - 1)
+    there = [there_x[0], there_x[1], there_y[0], there_y[1]]
+    there += [there_x[i] & there_y[j] for i in range(2) for j in range(2)]
+    for other, ok in zip(others, there):
+        @pl.when(ok)
+        def _():
+            pl.semaphore_signal(barrier, inc=1, device_id=other, device_id_type=MESH)
 
     loads = {}
     for at, (name, src, dst) in enumerate(
@@ -42,9 +48,6 @@
     m0, m1, m2, m3 = medium[0], medium[1], medium[2], medium[3]
     c = 0.05 * medium[4]
     al = 0.33 + c
-    inside = [gx > 0, gx < nx - 1]
-    mx = [jnp.where(inside[s], 1.0, 0.0).astype(jnp.float32) for s in range(2)]
-    my = [jnp.where(t, 1.0, 0.0).astype(jnp.float32) for t in (gy > 0, gy < ny - 1)]
 
     lane = lax.broadcasted_iota(jnp.int32, (8, LANES), 1)
     first, last = lane == 0, lane == LANES - 1
@@ -97,12 +100,31 @@
     def line(h, y):
         return pl.ds(h * Y + y, X, stride=H * Y)
 
-    def send(at, src, dst, device):
-        copy = pltpu.make_async_remote_copy(
-            src_ref=src, dst_ref=dst, send_sem=send_sem.at[at], recv_sem=recv_sem.at[at],
-            device_id=device, device_id_type=MESH)
-        copy.start()
-        return copy
+    def send(at, src, dst, device, ok, back):
+        def describe():
+            return pltpu.make_async_remote_copy(
+                src_ref=src, dst_ref=dst, send_sem=send_sem.at[at], recv_sem=recv_sem.at[at],
+                device_id=device, device_id_type=MESH)
+
+        @pl.when(ok)
+        def _():
+            describe().start()
+
+        return describe, ok, back
+
+    def sent(entry):
+        describe, ok, _ = entry
+
+        @pl.when(ok)
+        def _():
+            describe().wait_send()
+
+    def arrived(entry):
+        describe, _, back = entry
+
+        @pl.when(back)
+        def _():
+            describe().wait_recv()
 
     def clear(x):
         for h in range(H):
@@ -144,14 +166,43 @@
 
     loop(X, admit)
 
+    for s in range(2):
+        @pl.when(jnp.logical_not(there_x[s]))
+        def _():
+            def none(j):
+                for h in range(H):
+                    xr[0, 2, s, h, rows(j), :] = zero
+                    for e in range(2):
+                        for field in range(2):
+                            xr[e, field, s, h, rows(j), :] = zero
+
+            loop(T, none)
+
+        @pl.when(jnp.logical_not(there_y[s]))
+        def _():
+            blank = jnp.zeros((X, LANES), jnp.float32)
+            for h in range(H):
+                yr[0, s, 1, h] = blank
+                for e in range(2):
+                    yr[e, s, 0, h] = blank
+                    yrg[e, s, h] = blank
+
+        for t in range(2):
+            @pl.when(jnp.logical_not(there_x[s] & there_y[t]))
+            def _():
+                for e in range(2):
+                    cr[e, s, t] = zero
+
     pending = {}
     message = iter(range(64))
-    pl.semaphore_wait(barrier, len(others))
+    beside_x = jnp.where(gx > 0, 1, 0) + jnp.where(gx < nx - 1, 1, 0)
+    beside_y = jnp.where(gy > 0, 1, 0) + jnp.where(gy < ny - 1, 1, 0)
+    pl.semaphore_wait(barrier, beside_x + beside_y + beside_x * beside_y)
 
     def send_planes(e):
         for s in range(2):
             pending["w", e, s] = send(
-                next(message), even.at[1 if s == 0 else X, :, pl.ds(PAD, Y), :], xr.at[e, 0, 1 - s], (xs[s], gy))
+                next(message), even.at[1 if s == 0 else X, :, pl.ds(PAD, Y), :], xr.at[e, 0, 1 - s], (xs[s], gy), there_x[s], there_x[1 - s])
 
     def send_corners(e):
         for s in range(2):
@@ -159,7 +210,7 @@
                 for h in range(H):
                     cs[e, s, t, pl.ds(h, 1), :] = even[1 if s == 0 else X, h, pl.ds(PAD + edge_rows(t), 1), :]
                 pending["c", e, s, t] = send(
-                    next(message), cs.at[e, s, t], cr.at[e, 1 - s, 1 - t], (xs[s], yside[t]))
+                    next(message), cs.at[e, s, t], cr.at[e, 1 - s, 1 - t], (xs[s], yside[t]), there_x[s] & there_y[t], there_x[1 - s] & there_y[1 - t])
 
     def send_lines(e):
         for t in range(2):
@@ -169,7 +220,7 @@
                     ys[e, t, 1, h] = flat_a[line(h, edge_rows(t)), :]
             fields = 2 if e == 0 else 1
             pending["y", e, t] = send(
-                next(message), ys.at[e, t, pl.ds(0, fields)], yr.at[e, 1 - t, pl.ds(0, fields)], (gx, yside[t]))
+                next(message), ys.at[e, t, pl.ds(0, fields)], yr.at[e, 1 - t, pl.ds(0, fields)], (gx, yside[t]), there_y[t], there_y[1 - t])
 
     for e in range(STEPS // 2):
         if e == 0:
@@ -178,7 +229,7 @@
             send_corners(e)
             for s in range(2):
                 pending["a", s] = send(
-                    next(message), adm.at[0 if s == 0 else X - 1], xr.at[0, 2, 1 - s], (xs[s], gy))
+                    next(message), adm.at[0 if s == 0 else X - 1], xr.at[0, 2, 1 - s], (xs[s], gy), there_x[s], there_x[1 - s])
             for name in ("o", "n"):
                 for copy in loads[name]:
                     copy.wait()
@@ -189,7 +240,7 @@
 
         loop(2, first_planes)
         for s in range(2):
-            pending["g", e, s] = send(next(message), gs.at[2 * e + s], xr.at[e, 1, 1 - s], (xs[s], gy))
+            pending["g", e, s] = send(next(message), gs.at[2 * e + s], xr.at[e, 1, 1 - s], (xs[s], gy), there_x[s], there_x[1 - s])
 
         if e > 0:
             def rest(i):
@@ -207,7 +258,7 @@
         for t in range(2):
             for h in range(H):
                 yg[e, t, h] = flat_odd[wline(h, edge_rows(t)), :]
-            pending["yg", e, t] = send(next(message), yg.at[e, t], yrg.at[e, 1 - t], (gx, yside[t]))
+            pending["yg", e, t] = send(next(message), yg.at[e, t], yrg.at[e, 1 - t], (gx, yside[t]), there_y[t], there_y[1 - t])
 
         def inner(i):
             for j in range(1, T - 1):
@@ -216,58 +267,58 @@
         loop(X - 4, inner, 2)
 
         for t in range(2):
-            pending["y", e, t].wait_recv()
-        for t in range(2):
-            for h in range(H):
-                add = flat_a[line(h, edge_rows(t)), :] * (my[t] * yr[e, t, 0, h])
+            arrived(pending["y", e, t])
+        for t in range(2):
+            for h in range(H):
+                add = flat_a[line(h, edge_rows(t)), :] * yr[e, t, 0, h]
                 flat_b[line(h, edge_rows(t)), :] = flat_b[line(h, edge_rows(t)), :] + add
                 flat_odd[wline(h, edge_rows(t)), :] = flat_odd[wline(h, edge_rows(t)), :] + al * add
         for t in range(2):
-            pending["yg", e, t].wait_recv()
+            arrived(pending["yg", e, t])
         for t in range(2):
             for h in range(H):
                 y = -1 if t == 0 else Y
-                flat_odd[wline(h, y), :] = my[t] * (yrg[e, t, h] + al * yr[0, t, 1, h] * ys[e, t, 0, h])
-        for s in range(2):
-            pending["w", e, s].wait_recv()
+                flat_odd[wline(h, y), :] = yrg[e, t, h] + al * yr[0, t, 1, h] * ys[e, t, 0, h]
+        for s in range(2):
+            arrived(pending["w", e, s])
         for s in range(2):
             x = 0 if s == 0 else X - 1
 
             def face(j, s=s, x=x, e=e):
                 for h in range(H):
-                    add = adm[x, h, rows(j), :] * (mx[s] * xr[e, 0, s, h, rows(j), :])
+                    add = adm[x, h, rows(j), :] * xr[e, 0, s, h, rows(j), :]
                     B[x, h, rows(j), :] = B[x, h, rows(j), :] + add
                     odd[x + 1, h, wrows(j), :] = odd[x + 1, h, wrows(j), :] + al * add
 
             loop(T, face, T)
         for s in range(2):
             if e == 0:
-                pending["a", s].wait_recv()
-            pending["g", e, s].wait_recv()
+                arrived(pending["a", s])
+            arrived(pending["g", e, s])
         for s in range(2):
             x, halo = (0, 0) if s == 0 else (X - 1, X + 1)
 
             def layer(j, s=s, x=x, halo=halo, e=e):
                 for h in range(H):
-                    odd[halo, h, wrows(j), :] = mx[s] * (
+                    odd[halo, h, wrows(j), :] = (
                         xr[e, 1, s, h, rows(j), :]
                         + al * xr[0, 2, s, h, rows(j), :] * even[x + 1, h, wrows(j), :])
 
             loop(T, layer, T)
         for s in range(2):
             for t in range(2):
-                pending["c", e, s, t].wait_recv()
+                arrived(pending["c", e, s, t])
         for s in range(2):
             x, halo = (1, 0) if s == 0 else (X, X + 1)
             for t in range(2):
                 y, over = (0, -1) if t == 0 else (Y - 1, Y)
                 for h in range(H):
-                    scaled = (mx[s] * my[t] * al) * cr[e, s, t, pl.ds(h, 1), :]
+                    scaled = al * cr[e, s, t, pl.ds(h, 1), :]
                     at = pl.ds(PAD + y, 1)
                     odd[halo, h, at, :] = odd[halo, h, at, :] + xr[0, 2, s, h, pl.ds(y, 1), :] * scaled
                     at = pl.ds(PAD + over, 1)
                     odd[x, h, at, :] = odd[x, h, at, :] + yr[0, t, 1, h, pl.ds(x - 1, 1), :] * scaled
-            pending["w", e, s].wait_send()
+            sent(pending["w", e, s])
 
         def ends(i):
             for j in range(T):
@@ -292,7 +343,7 @@
 
     for name, copy in pending.items():
         if name[0] != "w":
-            copy.wait_send()
+            sent(copy)
 
 
 def store_kernel(a, b, o, n, p_out, q_out, o_out, n_out, sems):

time: 26.2 us -> 22.5 us (0.86)
  the two profiles are of different devices: /device:TPU:2 before, /device:TPU:26 now
where the time goes in v2:
time: 22.5 us; the launch traced here: 22.4 us
  Pallas kernels  21.8 us (97%)
  between operations  0.64 us (3%)
    pallas_call x1, Pallas kernels, per_device(): pl.pallas_call(functools.partial(steps_kernel, nx, ny), out_shape=[pltpu....  19.7 us
    pallas_call x1, Pallas kernels, per_device(): pl.pallas_call(store_kernel, out_shape=[jax.ShapeDtypeStruct((X, Y, Z), f...  2.07 us

profile of v2, /device:TPU:26, one launch (start us, length us, event | category | flops | bytes accessed | tf_op | source)
XLA Modules:
  0.0 22.4 jit_solution(10938395070104945202)
XLA Ops:
  0.6 19.7 %shard_map.102 = (f32[16,2,64,128]{3,2,1,0:T(8,128)S(1)}, f32[16,2,64,128]{3,2,1,0:T(8,128)S(1)}, f32[16,2,64,128]{3,2,1,0:T(8,128)S(1)}, f32[16,2,64,128]{3,2,1,0:T(8,128)S(1)}) custom-call(f32[16,64,256]{2,1,0:T(8,128)} %p_hbm.1, f32[16,64,256]{2,1,0:T(8,128)} %q_hbm.1, f32[16,64,256]{2,1,0:T(8,128)} %o_hbm.1, f32[16,64,256]{2,1,0:T(8,128)} %n_hbm.1, ...), custom_call_target="tpu_custom_call" | custom-call | tf_op jit(solution)/shard_map/pallas_call | solution.py:370
  20.3 2.1 %shard_map.103 = (f32[16,64,256]{2,1,0:T(8,128)}, f32[16,64,256]{2,1,0:T(8,128)}, f32[16,64,256]{2,1,0:T(8,128)}, f32[16,64,256]{2,1,0:T(8,128)}) custom-call(f32[16,2,64,128]{3,2,1,0:T(8,128)S(1)} %get-tuple-element.8.a, f32[16,2,64,128]{3,2,1,0:T(8,128)S(1)} %get-tuple-element.9.b, f32[16,2,64,128]{3,2,1,0:T(8,128)S(1)} %get-tuple-element.10.o, ...), custom_call_target="tpu_custom_call" | custom-call | tf_op jit(solution)/shard_map/pallas_call | solution.py:395

commit v3 on v0

v3 whole, which is shorter than its diff:
```python
import functools

import jax
import jax.numpy as jnp
from jax import lax
from jax.experimental import pallas as pl
from jax.experimental.pallas import tpu as pltpu
from jax.sharding import PartitionSpec as P

STEPS = 4
NCLASS = 8
MESH = pl.DeviceIdType.MESH
LANES = 128
PAD = 8
WIDE = 16
OUT = 3


def steps_kernel(nx, ny, p_hbm, q_hbm, o_hbm, n_hbm, c_hbm, wall, medium, A, B, O, N,
                 cls, adm, even, odd, dA, dB, dO, dN, dE, dD,
                 fs, ys, ya, xe, cs0, cs1, fr, xa, yr, yar, xer, cr0, cr1,
                 load_sem, send_sem, recv_sem):
    X, H, Y, _ = A.shape
    T = Y // 8
    gx, gy = lax.axis_index("gx"), lax.axis_index("gy")
    xs = (lax.rem(gx + nx - 1, nx), lax.rem(gx + 1, nx))
    yside = (lax.rem(gy + ny - 1, ny), lax.rem(gy + 1, ny))
    there_x = (gx > 0, gx < nx - 1)
    there_y = (gy > 0, gy < ny - 1)
    sides = [(s, t) for s in range(2) for t in range(2)]

    barrier = pltpu.get_barrier_semaphore()
    others = [((xs[s], gy), there_x[s]) for s in range(2)]
    others += [((gx, yside[t]), there_y[t]) for t in range(2)]
    others += [((xs[s], yside[t]), there_x[s] & there_y[t]) for s, t in sides]
    for other, ok in others:
        @pl.when(ok)
        def _():
            pl.semaphore_signal(barrier, inc=1, device_id=other, device_id_type=MESH)

    loads = {}
    for at, (name, src, dst) in enumerate(
        (("p", p_hbm, A), ("q", q_hbm, B), ("c", c_hbm, cls), ("o", o_hbm, O), ("n", n_hbm, N))
    ):
        loads[name] = [
            pltpu.make_async_copy(src.at[:, :, pl.ds(LANES * h, LANES)], dst.at[:, h], load_sem.at[at, h])
            for h in range(H)
        ]
        for copy in loads[name]:
            copy.start()

    def loaded(name):
        for copy in loads[name]:
            copy.wait()

    m0, m1, m2, m3 = medium[0], medium[1], medium[2], medium[3]
    c = 0.05 * medium[4]
    al = 0.33 + c

    lane = lax.broadcasted_iota(jnp.int32, (8, LANES), 1)
    first, last = lane == 0, lane == LANES - 1
    zero = jnp.zeros((8, LANES), jnp.float32)

    def loop(count, body, unroll=1):
        lax.fori_loop(0, count, lambda i, carry: (body(i), carry)[1], 0, unroll=unroll)

    def rows(j, pad=0, by=0):
        return pl.ds(pad + 8 * j + by, 8)

    def depth_x(s, d):
        return d if s == 0 else X - 1 - d

    def depth_y(t, d):
        return d if t == 0 else Y - 1 - d

    def advance(x, j, now, then, oxy, nit, xo, pad, src, wx, wpad):
        w = [src[x + wx, h, rows(j, wpad), :] for h in range(H)]
        down = [pltpu.roll(v, 1, 1) for v in w]
        up = [pltpu.roll(v, LANES - 1, 1) for v in w]
        below = [jnp.where(first, 0.0, down[0]), jnp.where(first, down[0], down[1])]
        above = [jnp.where(last, up[1], up[0]), jnp.where(last, 0.0, up[1])]
        result = []
        for h in range(H):
            at = (x + xo, h, rows(j, pad), slice(None))
            p, q = now[at], then[at]
            total = src[x + wx - 1, h, rows(j, wpad), :] + src[x + wx + 1, h, rows(j, wpad), :]
            total = total + (src[x + wx, h, rows(j, wpad, -1), :] + src[x + wx, h, rows(j, wpad, 1), :])
            total = total + (below[h] + above[h])
            d = p - q
            o = m0 * oxy[at] + m1 * d
            n = m2 * nit[at] + m3 * d
            new = q + adm[x + OUT, h, rows(j, PAD), :] * ((total - 6.0 * w[h]) + (2.0 * d - (o + n)))
            result.append((h, at, p, new, o, n))
        return result

    def alone(x, tiles, now, then, src, dst, keep=None):
        for j0 in range(0, len(tiles), 2):
            done = [(j, r) for j in tiles[j0:j0 + 2] for r in advance(x, j, now, then, O, N, 0, 0, src, 1, PAD)]
            for j, (h, at, p, new, o, n) in done:
                then[at] = new
                O[at] = o
                N[at] = n
                if dst is not None:
                    v = al * new - c * p
                    dst[x + 1, h, rows(j, PAD), :] = v
                    if keep is not None:
                        keep[h, rows(j), :] = v

    def coupled(x, tiles, now, then, src, dst):
        for j0 in range(0, len(tiles), 2):
            done = [(j, r) for j in tiles[j0:j0 + 2]
                    for r in advance(x, j, now, then, dO, dN, OUT, WIDE, src, OUT, WIDE)]
            for j, (h, at, p, new, o, n) in done:
                if dst is not None:
                    then[at] = new
                    dO[at] = o
                    dN[at] = n
                    dst[at] = al * new - c * p
                else:
                    to = (x, h, rows(j), slice(None))
                    A[to] = A[to] + new
                    B[to] = B[to] + p
                    O[to] = O[to] + o
                    N[to] = N[to] + n

    def flat(ref):
        planes, halves, height, _ = ref.shape
        return ref.reshape(planes * halves * height, LANES)

    def line(ref, h, y, xo, pad):
        height = ref.shape[2]
        return pl.ds((xo * H + h) * height + pad + y, X, stride=H * height)

    messages = iter(range(64))

    def send(src, dst, device, ok, back):
        at = next(messages)

        def describe():
            return pltpu.make_async_remote_copy(
                src_ref=src, dst_ref=dst, send_sem=send_sem.at[at], recv_sem=recv_sem.at[at],
                device_id=device, device_id_type=MESH)

        @pl.when(ok)
        def _():
            describe().start()

        return describe, ok, back

    def sent(entry):
        @pl.when(entry[1])
        def _():
            entry[0]().wait_send()

    def arrived(entry):
        @pl.when(entry[2])
        def _():
            entry[0]().wait_recv()

    def clear(x):
        for ref in (dE, dD, dA, dB, dO, dN):
            for h in range(H):
                for j in range(-2, T + 2):
                    ref[x, h, rows(j, WIDE), :] = zero
        for h in range(H):
            adm[x, h, rows(-1, PAD), :] = zero
            adm[x, h, rows(T, PAD), :] = zero

    def clear_own(x):
        for h in range(H):
            for ref in (even, odd):
                ref[x, h, rows(-1, PAD), :] = zero
                ref[x, h, rows(T, PAD), :] = zero

    def clear_faces(j):
        for h in range(H):
            for ref in (even, odd):
                for x in (0, X + 1):
                    ref[x, h, rows(j, PAD), :] = zero
            for x in (0, X + 2 * OUT - 1):
                adm[x, h, rows(j, PAD), :] = zero

    loop(X + 2 * OUT, clear)
    loop(X + 2, clear_own)
    loop(T, clear_faces)
    blank = jnp.zeros((X, LANES), jnp.float32)
    for s in range(2):
        @pl.when(jnp.logical_not(there_x[s]))
        def _():
            def none(j):
                for h in range(H):
                    for k in range(STEPS):
                        fr[k, s, h, rows(j), :] = zero
                    for d in range(2):
                        xa[s, d, h, rows(j), :] = zero

            loop(T, none)
            xer[s] = zero

        @pl.when(jnp.logical_not(there_y[s]))
        def _():
            for h in range(H):
                for k in range(1, STEPS):
                    yr[k, s, h] = blank
                for f in range(3):
                    yar[s, pl.ds((f * H + h) * X, X), :] = blank
            yar[s, pl.ds(3 * H * X, 8), :] = zero

        for t in range(2):
            @pl.when(jnp.logical_not(there_x[s] & there_y[t]))
            def _():
                cr0[s, t, pl.ds(0, 8), :] = zero
                cr0[s, t, pl.ds(8, 8), :] = zero
                cr1[0, s, t] = zero
                cr1[1, s, t] = zero

    loaded("p")
    loaded("q")

    def first_w(x, keep=None):
        for j in range(T):
            for h in range(H):
                v = al * A[x, h, rows(j), :] - c * B[x, h, rows(j), :]
                even[x + 1, h, rows(j, PAD), :] = v
                if keep is not None:
                    keep[h, rows(j), :] = v

    table = [1.0 / (1.0 + 0.5 * jnp.full((8, LANES), wall[k], jnp.float32)) for k in range(1, NCLASS)]

    def admit(x):
        for j in range(T):
            for h in range(H):
                kind = cls[x, h, rows(j), :]
                a = jnp.ones((8, LANES), jnp.float32)
                for k in range(1, NCLASS):
                    a = jnp.where(kind == k, table[k - 1], a)
                adm[x + OUT, h, rows(j, PAD), :] = a

    loop(2, lambda s: first_w((X - 1) * s, fs.at[0, s]))
    loop(X - 2, lambda i: first_w(i + 1), 2)
    loaded("c")
    loop(X, admit, 2)

    def row(ref, x, h, y, xo, pad):
        return ref[x + xo, h, pl.ds(pad + y, 1), :]

    flat_a = flat(adm)
    for t in range(2):
        for h in range(H):
            ya[t, pl.ds(h * X, X), :] = flat(even)[line(even, h, depth_y(t, 0), 1, PAD), :]
            for d in range(2):
                ya[t, pl.ds(((d + 1) * H + h) * X, X), :] = flat_a[line(adm, h, depth_y(t, d), OUT, PAD), :]
            for s in range(2):
                ya[t, pl.ds(3 * H * X + s * H + h, 1), :] = row(even, depth_x(s, 0), h, depth_y(t, 1), 1, PAD)
                ya[t, pl.ds(3 * H * X + 2 * H + s * H + h, 1), :] = row(
                    adm, depth_x(s, 0), h, depth_y(t, 2), OUT, PAD)
    near = ((0, 0), (1, 0), (0, 1), (2, 0), (0, 2))
    for s in range(2):
        for t in range(2):
            for h in range(H):
                xe[s, pl.ds(t * H + h, 1), :] = row(even, depth_x(s, 1), h, depth_y(t, 0), 1, PAD)
                xe[s, pl.ds(2 * H + t * H + h, 1), :] = row(adm, depth_x(s, 2), h, depth_y(t, 0), OUT, PAD)
                for i, (dx, dy) in enumerate(near):
                    cs0[s, t, pl.ds(i * H + h, 1), :] = row(even, depth_x(s, dx), h, depth_y(t, dy), 1, PAD)
                for i, (dx, dy) in enumerate(near[:3]):
                    cs0[s, t, pl.ds((5 + i) * H + h, 1), :] = row(adm, depth_x(s, dx), h, depth_y(t, dy), OUT, PAD)

    beside_x = jnp.where(gx > 0, 1, 0) + jnp.where(gx < nx - 1, 1, 0)
    beside_y = jnp.where(gy > 0, 1, 0) + jnp.where(gy < ny - 1, 1, 0)
    pl.semaphore_wait(barrier, beside_x + beside_y + beside_x * beside_y)

    def to_x(s, src, dst):
        return send(src, dst, (xs[s], gy), there_x[s], there_x[1 - s])

    def to_y(t, src, dst):
        return send(src, dst, (gx, yside[t]), there_y[t], there_y[1 - t])

    def to_corner(s, t, src, dst):
        return send(src, dst, (xs[s], yside[t]), there_x[s] & there_y[t], there_x[1 - s] & there_y[1 - t])

    pending = [[] for _ in range(STEPS)]
    for s in range(2):
        pending[0].append(to_x(s, fs.at[0, s], fr.at[0, 1 - s]))
    for s in range(2):
        pending[0].append(to_x(s, xe.at[s], xer.at[1 - s]))
    for t in range(2):
        pending[0].append(to_y(t, ya.at[t], yar.at[1 - t]))
    for s, t in sides:
        pending[0].append(to_corner(s, t, cs0.at[s, t], cr0.at[1 - s, 1 - t]))
    for s in range(2):
        for d in range(2):
            pending[0].append(to_x(
                s, adm.at[depth_x(s, d) + OUT, :, pl.ds(PAD, Y), :], xa.at[1 - s, d]))
    loaded("o")
    loaded("n")

    every = list(range(T))
    for k in range(STEPS):
        now, then = (A, B) if k % 2 == 0 else (B, A)
        src, dst = (even, odd) if k % 2 == 0 else (odd, even)
        if k == STEPS - 1:
            loop(X, lambda x: alone(x, every, now, then, src, None), 4)
            break
        loop(2, lambda s: alone((X - 1) * s, every, now, then, src, dst, fs.at[k + 1, s]), 2)
        for s in range(2):
            pending[k + 1].append(to_x(s, fs.at[k + 1, s], fr.at[k + 1, 1 - s]))
        loop(X - 2, lambda i: alone(i + 1, every, now, then, src, dst), 7)
        for t in range(2):
            for h in range(H):
                ys[k + 1, t, h] = flat(dst)[line(dst, h, depth_y(t, 0), 1, PAD), :]
            pending[k + 1].append(to_y(t, ys.at[k + 1, t], yr.at[k + 1, 1 - t]))
        if k < 2:
            for s, t in sides:
                for h in range(H):
                    for i, (dx, dy) in enumerate(near[:3 if k == 0 else 1]):
                        cs1[k, s, t, pl.ds(i * H + h, 1), :] = row(dst, depth_x(s, dx), h, depth_y(t, dy), 1, PAD)
                pending[k + 1].append(to_corner(s, t, cs1.at[k, s, t], cr1.at[k, 1 - s, 1 - t]))

    def own_rows(k, t, h):
        return ya[t, pl.ds(h * X, X), :] if k == 0 else ys[k, t, h]

    def their_rows(k, t, h):
        return yar[t, pl.ds(h * X, X), :] if k == 0 else yr[k, t, h]

    def sources(k, then, dst):
        def plane(s, d, value):
            x = depth_x(s, d) + OUT

            def part(j):
                for h in range(H):
                    add = adm[x, h, rows(j, PAD), :] * value[h, rows(j), :]
                    then[x, h, rows(j, WIDE), :] = then[x, h, rows(j, WIDE), :] + add
                    dst[x, h, rows(j, WIDE), :] = dst[x, h, rows(j, WIDE), :] + al * add

            loop(T, part, T)

        def lines(y, h, value):
            add = flat_a[line(adm, h, y, OUT, PAD), :] * value
            for ref, scale in ((then, 1.0), (dst, al)):
                at = line(ref, h, y, OUT, WIDE)
                flat(ref)[at, :] = flat(ref)[at, :] + scale * add

        def cell(s, t, dx, dy, h, value):
            x, y = depth_x(s, dx) + OUT, depth_y(t, dy)
            add = adm[x, h, pl.ds(PAD + y, 1), :] * value
            at = pl.ds(WIDE + y, 1)
            then[x, h, at, :] = then[x, h, at, :] + add
            dst[x, h, at, :] = dst[x, h, at, :] + al * add

        for s in range(2):
            plane(s, 0, fr.at[k, s])
            plane(s, -1, fs.at[k, s])
        for t in range(2):
            for h in range(H):
                lines(depth_y(t, 0), h, their_rows(k, t, h))
                lines(depth_y(t, -1), h, own_rows(k, t, h))
        for s, t in sides:
            diagonal = cr0.at[s, t] if k == 0 else cr1.at[k - 1, s, t]
            for h in range(H):
                def at(i):
                    return diagonal[pl.ds(i * H + h, 1), :]

                cell(s, t, -1, 0, h, at(0))
                cell(s, t, 0, -1, h, at(0))
                if k < 2:
                    cell(s, t, -2, 0, h, at(1))
                    cell(s, t, 0, -2, h, at(2))
                    beside = fr[k, s, h, pl.ds(depth_y(t, 0), 1), :]
                    if k == 0:
                        beside = beside + yar[t, pl.ds(h * X + depth_x(s, 0), 1), :]
                    else:
                        beside = beside + yr[k, t, h, pl.ds(depth_x(s, 0), 1), :]
                    cell(s, t, -1, -1, h, beside)
                if k == 0:
                    cell(s, t, -3, 0, h, at(3))
                    cell(s, t, 0, -3, h, at(4))
                    cell(s, t, -2, -1, h, xer[s, pl.ds(t * H + h, 1), :])
                    cell(s, t, -1, -2, h, yar[t, pl.ds(3 * H * X + s * H + h, 1), :])

    for entry in pending[0]:
        arrived(entry)
    for s in range(2):
        for d in range(2):
            def place(j, s=s, d=d):
                for h in range(H):
                    adm[depth_x(s, -1 - d) + OUT, h, rows(j, PAD), :] = xa[s, d, h, rows(j), :]

            loop(T, place, T)
    for t in range(2):
        for h in range(H):
            for d in range(2):
                flat_a[line(adm, h, depth_y(t, -1 - d), OUT, PAD), :] = yar[t, pl.ds(((d + 1) * H + h) * X, X), :]
            for s in range(2):
                def put(dx, dy, value, s=s, t=t, h=h):
                    adm[depth_x(s, dx) + OUT, h, pl.ds(PAD + depth_y(t, dy), 1), :] = value

                put(0, -3, yar[t, pl.ds(3 * H * X + 2 * H + s * H + h, 1), :])
                put(-3, 0, xer[s, pl.ds(2 * H + t * H + h, 1), :])
                for i, (dx, dy) in enumerate(near[:3]):
                    put(-1 - dx, -1 - dy, cr0[s, t, pl.ds((5 + i) * H + h, 1), :])
    sources(0, dB, dD)

    around = [-1, 0, T - 1, T]
    full = list(range(-1, T + 1))
    frames = {
        1: [(-2, every), (-1, full), (0, full), (1, full)],
        2: [(-1, every), (0, full), (1, full), (2, full)],
        3: [(0, every), (1, every), (2, every), (3, every)],
    }
    for k in range(1, STEPS):
        now, then = (dA, dB) if k % 2 == 0 else (dB, dA)
        src, dst = (dE, dD) if k % 2 == 0 else (dD, dE)
        last_step = k == STEPS - 1

        def faces(s):
            for d, tiles in frames[k]:
                coupled(d + s * (X - 1 - 2 * d), tiles, now, then, src, None if last_step else dst)

        loop(2, faces)
        inner = k + 1
        middle = [0, T - 1] if last_step else around
        loop(X - 2 * inner, lambda i: coupled(i + inner, middle, now, then, src, None if last_step else dst), 2)
        for entry in pending[k]:
            arrived(entry)
        if not last_step:
            sources(k, then, dst)

    for s in range(2):
        x = depth_x(s, 0)

        def final(j, s=s, x=x):
            for h in range(H):
                A[x, h, rows(j), :] = A[x, h, rows(j), :] + (
                    adm[x + OUT, h, rows(j, PAD), :] * fr[STEPS - 1, s, h, rows(j), :])

        loop(T, final, T)
    for t in range(2):
        for h in range(H):
            at = line(A, h, depth_y(t, 0), 0, 0)
            flat(A)[at, :] = flat(A)[at, :] + (
                flat_a[line(adm, h, depth_y(t, 0), OUT, PAD), :] * yr[STEPS - 1, t, h])

    for group in pending:
        for entry in group:
            sent(entry)


def store_kernel(a, b, o, n, p_out, q_out, o_out, n_out, sems):
    copies = [
        pltpu.make_async_copy(src.at[:, h], dst.at[:, :, pl.ds(LANES * h, LANES)], sems.at[at, h])
        for at, (src, dst) in enumerate(((a, p_out), (b, q_out), (o, o_out), (n, n_out)))
        for h in range(2)
    ]
    for copy in copies:
        copy.start()
    for copy in copies:
        copy.wait()


def per_device(nx, ny, pressure, previous, oxygen_aux, nitrogen_aux, cell_class, wall_admittance, medium):
    X, Y, Z = pressure.shape
    H = Z // LANES
    split = (X, H, Y, LANES)
    padded = (X + 2, H, Y + 2 * PAD, LANES)
    wide = (X + 2 * OUT, H, Y + 2 * WIDE, LANES)
    hbm = pl.BlockSpec(memory_space=pl.ANY)
    vmem = pl.BlockSpec(memory_space=pltpu.VMEM)
    smem = pl.BlockSpec(memory_space=pltpu.SMEM)
    f32 = jnp.float32
    rows_y = 3 * H * X + 8
    state = pl.pallas_call(
        functools.partial(steps_kernel, nx, ny),
        out_shape=[pltpu.VMEM(split, f32)] * 4,
        in_specs=[hbm] * 5 + [smem] * 2,
        out_specs=[vmem] * 4,
        scratch_shapes=[
            pltpu.VMEM(split, jnp.int32),
            pltpu.VMEM((X + 2 * OUT, H, Y + 2 * PAD, LANES), f32),
            pltpu.VMEM(padded, f32),
            pltpu.VMEM(padded, f32),
            *[pltpu.VMEM(wide, f32)] * 6,
            pltpu.VMEM((STEPS, 2, H, Y, LANES), f32),
            pltpu.VMEM((STEPS, 2, H, X, LANES), f32),
            pltpu.VMEM((2, rows_y, LANES), f32),
            pltpu.VMEM((2, 8, LANES), f32),
            pltpu.VMEM((2, 2, 16, LANES), f32),
            pltpu.VMEM((2, 2, 2, 8, LANES), f32),
            pltpu.VMEM((STEPS, 2, H, Y, LANES), f32),
            pltpu.VMEM((2, 2, H, Y, LANES), f32),
            pltpu.VMEM((STEPS, 2, H, X, LANES), f32),
            pltpu.VMEM((2, rows_y, LANES), f32),
            pltpu.VMEM((2, 8, LANES), f32),
            pltpu.VMEM((2, 2, 16, LANES), f32),
            pltpu.VMEM((2, 2, 2, 8, LANES), f32),
            pltpu.SemaphoreType.DMA((5, 2)),
            pltpu.SemaphoreType.DMA((40,)),
            pltpu.SemaphoreType.DMA((40,)),
        ],
        compiler_params=pltpu.CompilerParams(
            collective_id=0, has_side_effects=True, vmem_limit_bytes=56 << 20),
    )(pressure, previous, oxygen_aux, nitrogen_aux, cell_class, wall_admittance, medium)
    out = pl.pallas_call(
        store_kernel,
        out_shape=[jax.ShapeDtypeStruct((X, Y, Z), f32)] * 4,
        in_specs=[vmem] * 4,
        out_specs=[hbm] * 4,
        scratch_shapes=[pltpu.SemaphoreType.DMA((4, 2))],
        compiler_params=pltpu.CompilerParams(vmem_limit_bytes=16 << 20),
    )(*state)
    return tuple(out)


def solution(mesh):
    field = P("gx", "gy", None)
    return jax.shard_map(
        functools.partial(per_device, mesh.shape["gx"], mesh.shape["gy"]),
        mesh=mesh,
        in_specs=(field,) * 5 + (P(), P()),
        out_specs=(field,) * 4,
        check_vma=False,
    )
```

time: 127 us -> 20.7 us (0.16); the launches traced: 125 us -> 20.6 us
  starting transfers between devices: 55.7 us -> 0 us
  other arithmetic: 44.6 us -> 0 us
  Pallas kernels: 0 us -> 20 us
  waiting for transfers between devices: 17.4 us -> 0 us
  local copies, waits for them, and re-layouts: 5.07 us -> 0 us
    ppermute x16 -> x0, starting transfers between devices: 55.7 us -> none  [the longest x8 37.7 us: extended(): after = lax.ppermute(first, axis, down)]
    div x4 -> x0, other arithmetic: 41.2 us -> none  [advance(): return (update / (1.0 + boundary), current, oxygen, nitrogen)]
    pallas_call x0 -> x2, Pallas kernels: none -> 20 us  [the longest x1 17.9 us: per_device(): pl.pallas_call(functools.partial(steps_kernel, nx, ny), out_shape=[pltpu....]
    ppermute x16 -> x0, waiting for transfers between devices: 17.4 us -> none  [the longest x8 15.3 us: extended(): after = lax.ppermute(first, axis, down)]
    slice x10 -> x0, local copies, waits for them, and re-layouts: 3.09 us -> none  [the longest x1 1.57 us: lookup(): damping = jnp.where(classes == number, wall_admittance[number], damping)]
    unnamed x14 -> x0, local copies, waits for them, and re-layouts: 1.62 us -> none
    slice x8 -> x0, other arithmetic: 1.37 us -> none  [extended(): last = lax.slice_in_dim(x, length - width, length, axis=dim)]
    concatenate x4 -> x0, other arithmetic: 1.33 us -> none  [extended(): x = jnp.concatenate([before, x, after], axis=dim)]
  transfers between devices with their start and end apart: 16 -> 0, of which waited for: 11 -> 0; matrix products, arithmetic and copies ran while one was open for 2% -> 0% of each run, Pallas kernels for 0% -> 0%
where the time goes in v3:
time: 20.7 us; the launch traced here: 20.6 us
  Pallas kernels  20 us (97%)
  between operations  0.64 us (3%)
    pallas_call x1, Pallas kernels, per_device(): pl.pallas_call(functools.partial(steps_kernel, nx, ny), out_shape=[pltpu....  17.9 us
    pallas_call x1, Pallas kernels, per_device(): pl.pallas_call(store_kernel, out_shape=[jax.ShapeDtypeStruct((X, Y, Z), f...  2.07 us

profile of v3, /device:TPU:26, one launch (start us, length us, event | category | flops | bytes accessed | tf_op | source)
XLA Modules:
  0.0 20.6 jit_solution(15074323136621145938)
XLA Ops:
  0.6 17.9 %shard_map.102 = (f32[16,2,64,128]{3,2,1,0:T(8,128)S(1)}, f32[16,2,64,128]{3,2,1,0:T(8,128)S(1)}, f32[16,2,64,128]{3,2,1,0:T(8,128)S(1)}, f32[16,2,64,128]{3,2,1,0:T(8,128)S(1)}) custom-call(f32[16,64,256]{2,1,0:T(8,128)} %p_hbm.1, f32[16,64,256]{2,1,0:T(8,128)} %q_hbm.1, f32[16,64,256]{2,1,0:T(8,128)} %o_hbm.1, f32[16,64,256]{2,1,0:T(8,128)} %n_hbm.1, ...), custom_call_target="tpu_custom_call" | custom-call | tf_op jit(solution)/shard_map/pallas_call | solution.py:471
  18.5 2.1 %shard_map.103 = (f32[16,64,256]{2,1,0:T(8,128)}, f32[16,64,256]{2,1,0:T(8,128)}, f32[16,64,256]{2,1,0:T(8,128)}, f32[16,64,256]{2,1,0:T(8,128)}) custom-call(f32[16,2,64,128]{3,2,1,0:T(8,128)S(1)} %get-tuple-element.8.a, f32[16,2,64,128]{3,2,1,0:T(8,128)S(1)} %get-tuple-element.9.b, f32[16,2,64,128]{3,2,1,0:T(8,128)S(1)} %get-tuple-element.10.o, ...), custom_call_target="tpu_custom_call" | custom-call | tf_op jit(solution)/shard_map/pallas_call | solution.py:502

commit v4 on v3

v4 whole, which is shorter than its diff:
```python
import functools

import jax
import jax.numpy as jnp
from jax import lax
from jax.experimental import pallas as pl
from jax.experimental.pallas import tpu as pltpu
from jax.sharding import PartitionSpec as P

STEPS = 4
NCLASS = 8
MESH = pl.DeviceIdType.MESH
LANES = 128
PAD = 8
WIDE = 16
OUT = 3


def steps_kernel(nx, ny, p_hbm, q_hbm, o_hbm, n_hbm, c_hbm, wall, medium, A, B, O, N,
                 cls, adm, even, odd, dA, dB, dO, dN, dE, dD,
                 x0, fs, ys, ya, cs, x0r, fr, yr, yar, cr,
                 load_sem, send_sem, recv_sem):
    X, H, Y, _ = A.shape
    T = Y // 8
    gx, gy = lax.axis_index("gx"), lax.axis_index("gy")
    xs = (lax.rem(gx + nx - 1, nx), lax.rem(gx + 1, nx))
    yside = (lax.rem(gy + ny - 1, ny), lax.rem(gy + 1, ny))
    there_x = (gx > 0, gx < nx - 1)
    there_y = (gy > 0, gy < ny - 1)
    sides = [(s, t) for s in range(2) for t in range(2)]

    barrier = pltpu.get_barrier_semaphore()
    others = [((xs[s], gy), there_x[s]) for s in range(2)]
    others += [((gx, yside[t]), there_y[t]) for t in range(2)]
    others += [((xs[s], yside[t]), there_x[s] & there_y[t]) for s, t in sides]
    for other, ok in others[::-1]:
        @pl.when(ok)
        def _():
            pl.semaphore_signal(barrier, inc=1, device_id=other, device_id_type=MESH)

    quarter = X // 4
    chunks = {"ends": ((0, quarter), (X - quarter, quarter)), "middle": ((quarter, X - 2 * quarter),)}
    groups = (("p", "q"), ("c",), ("o", "n"))
    source = {"p": (p_hbm, A), "q": (q_hbm, B), "c": (c_hbm, cls), "o": (o_hbm, O), "n": (n_hbm, N)}
    order = [(names, part) for part in ("ends", "middle") for names in groups]
    for at, (names, part) in enumerate(order):
        for name in names:
            src, dst = source[name]
            for x, count in chunks[part]:
                for h in range(H):
                    pltpu.make_async_copy(
                        src.at[pl.ds(x, count), :, pl.ds(LANES * h, LANES)],
                        dst.at[pl.ds(x, count), h], load_sem.at[at]).start()

    def loaded(names, part):
        planes = len(names) * sum(count for _, count in chunks[part])
        whole = A.at[pl.ds(0, planes)]
        pltpu.make_async_copy(whole, whole, load_sem.at[order.index((names, part))]).wait()

    m0, m1, m2, m3 = medium[0], medium[1], medium[2], medium[3]
    c = 0.05 * medium[4]
    al = 0.33 + c

    lane = lax.broadcasted_iota(jnp.int32, (8, LANES), 1)
    first, last = lane == 0, lane == LANES - 1
    zero = jnp.zeros((8, LANES), jnp.float32)

    def loop(count, body, unroll=1):
        lax.fori_loop(0, count, lambda i, carry: (body(i), carry)[1], 0, unroll=unroll)

    def rows(j, pad=0, by=0):
        return pl.ds(pad + 8 * j + by, 8)

    def depth_x(s, d):
        return d if s == 0 else X - 1 - d

    def depth_y(t, d):
        return d if t == 0 else Y - 1 - d

    def advance(x, j, now, then, oxy, nit, xo, pad, src, wx, wpad, fresh=False, across=None):
        w = [src[x + wx, h, rows(j, wpad), :] for h in range(H)]
        down = [pltpu.roll(v, 1, 1) for v in w]
        up = [pltpu.roll(v, LANES - 1, 1) for v in w]
        below = [jnp.where(first, 0.0, down[0]), jnp.where(first, down[0], down[1])]
        above = [jnp.where(last, up[1], up[0]), jnp.where(last, 0.0, up[1])]
        result = []
        for h in range(H):
            at = (x + xo, h, rows(j, pad), slice(None))
            p = now[at]
            total = src[x + wx - 1, h, rows(j, wpad), :] + src[x + wx + 1, h, rows(j, wpad), :]
            total = total + (src[x + wx, h, rows(j, wpad, -1), :] + src[x + wx, h, rows(j, wpad, 1), :])
            total = total + (below[h] + above[h])
            if across is not None and 0 <= j < T:
                total = total + across(h, 8 * j, 8)
            a = adm[x + OUT, h, rows(j, PAD), :]
            if fresh:
                o, n = m1 * p, m3 * p
                new = a * ((total - 6.0 * w[h]) + (2.0 * p - (o + n)))
            else:
                q = then[at]
                d = p - q
                o = m0 * oxy[at] + m1 * d
                n = m2 * nit[at] + m3 * d
                new = q + a * ((total - 6.0 * w[h]) + (2.0 * d - (o + n)))
            result.append((h, at, p, new, o, n))
        return result

    def alone(x, tiles, now, then, src, dst, keep=None):
        for j0 in range(0, len(tiles), 2):
            done = [(j, r) for j in tiles[j0:j0 + 2] for r in advance(x, j, now, then, O, N, 0, 0, src, 1, PAD)]
            for j, (h, at, p, new, o, n) in done:
                then[at] = new
                O[at] = o
                N[at] = n
                if dst is not None:
                    v = al * new - c * p
                    dst[x + 1, h, rows(j, PAD), :] = v
                    if keep is not None:
                        keep[h, rows(j), :] = v

    def coupled(x, tiles, now, then, src, dst, fresh, across=None):
        for j0 in range(0, len(tiles), 2):
            done = [(j, r) for j in tiles[j0:j0 + 2]
                    for r in advance(x, j, now, then, dO, dN, OUT, WIDE, src, OUT, WIDE, fresh, across)]
            for j, (h, at, p, new, o, n) in done:
                if dst is not None:
                    then[at] = new
                    dO[at] = o
                    dN[at] = n
                    dst[at] = al * new - c * p
                else:
                    to = (x, h, rows(j), slice(None))
                    A[to] = A[to] + new
                    B[to] = B[to] + p
                    O[to] = O[to] + o
                    N[to] = N[to] + n

    def flat(ref):
        planes, halves, height, _ = ref.shape
        return ref.reshape(planes * halves * height, LANES)

    def line(ref, h, y, xo, pad):
        height = ref.shape[2]
        return pl.ds((xo * H + h) * height + pad + y, X, stride=H * height)

    messages = iter(range(recv_sem.shape[0]))
    in_flight = [[0, ok] for _, ok in others]

    def send(group, src, dst, device, ok, back, now):
        at = next(messages)
        in_flight[group][0] += src.size // LANES

        def describe():
            return pltpu.make_async_remote_copy(
                src_ref=src, dst_ref=dst, send_sem=send_sem.at[group], recv_sem=recv_sem.at[at],
                device_id=device, device_id_type=MESH)

        def start(when):
            @pl.when(ok & when)
            def _():
                describe().start()

        if now is None:
            held.append(start)
        else:
            start(now)
        return describe, back

    def arrived(entry):
        @pl.when(entry[1])
        def _():
            entry[0]().wait_recv()

    def clear(x):
        for ref in (dE, dD, dB):
            for h in range(H):
                for j in range(-2, T + 2):
                    ref[x, h, rows(j, WIDE), :] = zero
        for h in range(H):
            adm[x, h, rows(-1, PAD), :] = zero
            adm[x, h, rows(T, PAD), :] = zero

    def clear_next(i):
        for d in (2, 3):
            for ref in (dA, dO, dN):
                for h in range(H):
                    for j in range(T):
                        ref[d + i * (X - 1 - 2 * d) + OUT, h, rows(j, WIDE), :] = zero

    def clear_own(x):
        for h in range(H):
            for ref in (even, odd):
                ref[x, h, rows(-1, PAD), :] = zero
                ref[x, h, rows(T, PAD), :] = zero

    def clear_faces(j):
        for h in range(H):
            for ref in (even, odd):
                for x in (0, X + 1):
                    ref[x, h, rows(j, PAD), :] = zero
            for x in (0, X + 2 * OUT - 1):
                adm[x, h, rows(j, PAD), :] = zero

    loop(X + 2 * OUT, clear)
    loop(2, clear_next)
    loop(X + 2, clear_own)
    loop(T, clear_faces)
    blank = jnp.zeros((X, LANES), jnp.float32)
    for s in range(2):
        @pl.when(jnp.logical_not(there_x[s]))
        def _():
            def none(j):
                for h in range(H):
                    for k in range(STEPS - 1):
                        fr[k, s, h, rows(j), :] = zero

            def none_first(i):
                x0r[s, pl.ds(8 * i, 8), :] = zero

            loop(T, none)
            loop(x0.shape[1] // 8, none_first, 5)

        @pl.when(jnp.logical_not(there_y[s]))
        def _():
            for h in range(H):
                for k in range(STEPS - 1):
                    yr[k, s, h] = blank
                for f in range(3):
                    yar[s, pl.ds((f * H + h) * X, X), :] = blank
            yar[s, pl.ds(3 * H * X, 8), :] = zero

        for t in range(2):
            @pl.when(jnp.logical_not(there_x[s] & there_y[t]))
            def _():
                for i in range(3):
                    cr[s, t, pl.ds(8 * i, 8), :] = zero

    def first_w(x, keep=None):
        for j in range(T):
            for h in range(H):
                v = al * A[x, h, rows(j), :] - c * B[x, h, rows(j), :]
                even[x + 1, h, rows(j, PAD), :] = v
                if keep is not None:
                    x0[keep, rows(j, h * Y), :] = v

    extra = 2 * H * Y
    table = [1.0 / (1.0 + 0.5 * jnp.full((8, LANES), wall[k], jnp.float32)) for k in range(1, NCLASS)]

    def admit(x, keep=None, field=0):
        for j in range(T):
            for h in range(H):
                kind = cls[x, h, rows(j), :]
                a = jnp.ones((8, LANES), jnp.float32)
                for k in range(1, NCLASS):
                    a = jnp.where(kind == k, table[k - 1], a)
                adm[x + OUT, h, rows(j, PAD), :] = a
                if keep is not None:
                    x0[keep, rows(j, (field * H + h) * Y + (16 if field == 2 else 0)), :] = a

    def row(ref, x, h, y, xo, pad):
        return ref[x + xo, h, pl.ds(pad + y, 1), :]

    def to_x(s, src, dst, now):
        return send(s, src, dst, (xs[s], gy), there_x[s], there_x[1 - s], now)

    def to_y(t, src, dst, now):
        return send(2 + t, src, dst, (gx, yside[t]), there_y[t], there_y[1 - t], now)

    def to_corner(s, t, src, dst, now):
        return send(4 + 2 * s + t, src, dst, (xs[s], yside[t]), there_x[s] & there_y[t],
                    there_x[1 - s] & there_y[1 - t], now)

    ring = max(nx // 4, 1)
    early = (lax.rem(gx, ring) == 0) & (gx > 0)
    late = jnp.logical_not(early)
    held = []

    beside_x = jnp.where(gx > 0, 1, 0) + jnp.where(gx < nx - 1, 1, 0)
    beside_y = jnp.where(gy > 0, 1, 0) + jnp.where(gy < ny - 1, 1, 0)

    def greet(who):
        @pl.when(who)
        def _():
            pl.semaphore_wait(barrier, beside_x + beside_y + beside_x * beside_y)

    every = list(range(T))
    states = [(A, B, even, odd), (B, A, odd, even), (A, B, even, odd), (B, A, odd, None)]
    near = ((0, 0), (1, 0), (0, 1), (2, 0), (0, 2))

    def end(s, d):
        return d + s * (X - 1 - 2 * d)

    def lines_out(first_line, ref, xo, cells):
        for s, t in sides:
            for h in range(H):
                for i, (dx, dy) in enumerate(cells):
                    cs[s, t, pl.ds((first_line + i) * H + h, 1), :] = row(
                        ref, depth_x(s, dx), h, depth_y(t, dy), xo, PAD)

    def begin(s):
        first_w(end(s, 0), s)
        for d in range(1, quarter):
            first_w(end(s, d))

    def admit_ends(s):
        for d in range(quarter):
            admit(end(s, d), s if d < 2 else None, d + 1)

    loaded(("p", "q"), "ends")
    loop(2, begin)
    loaded(("c",), "ends")
    loop(2, admit_ends)
    lines_out(0, even, 1, near)
    lines_out(5, adm, OUT, near[:3])
    for s, t in sides:
        for h in range(H):
            x0[s, pl.ds(extra + t * H + h, 1), :] = row(even, depth_x(s, 1), h, depth_y(t, 0), 1, PAD)
            for i, d in enumerate((2, 1)):
                x0[s, pl.ds(extra + 2 * H * (i + 1) + t * H + h, 1), :] = row(
                    adm, depth_x(s, d), h, depth_y(t, 0), OUT, PAD)
    pending = [[] for _ in range(STEPS)]
    starts = []

    def both(make):
        held.clear()
        entry = make(None)
        held[0](late)
        starts.append(held[0])
        return entry

    greet(late)
    for s, t in sides:
        pending[0].append(both(lambda now: to_corner(
            s, t, cs.at[s, t, pl.ds(0, 16)], cr.at[1 - s, 1 - t, pl.ds(0, 16)], now)))
    second = []
    for part, rows_sent, entries in ((0, extra + 16, pending[0]), (extra + 16, H * Y, second)):
        for s in range(2):
            entries.append(both(lambda now: to_x(
                s, x0.at[s, pl.ds(part, rows_sent)], x0r.at[1 - s, pl.ds(part, rows_sent)], now)))
    loaded(("o", "n"), "ends")
    for k in range(3):
        def narrow(s, k=k):
            for d in range(3 - k):
                alone(end(s, d), every, *states[k], fs.at[k, s] if d == 0 else None)

        loop(2, narrow)
        if k < 2:
            lines_out(8 + 3 * k, states[k][3], 1, near[:3 if k == 0 else 1])
        if k == 1:
            for s, t in sides:
                pending[1].append(both(lambda now: to_corner(
                    s, t, cs.at[s, t, pl.ds(16, 8)], cr.at[1 - s, 1 - t, pl.ds(16, 8)], now)))
        for layer in ((), (0, 1), (2,))[k]:
            for s in range(2):
                pending[layer + 1].append(both(lambda now: to_x(s, fs.at[layer, s], fr.at[layer, 1 - s], now)))

    loaded(("p", "q"), "middle")
    loop(X - 2 * quarter, lambda i: first_w(i + quarter), 4)
    loaded(("c",), "middle")
    loop(X - 2 * quarter, lambda i: admit(i + quarter), 4)
    flat_a = flat(adm)
    for t in range(2):
        for h in range(H):
            for s in range(2):
                ya[t, pl.ds(3 * H * X + s * H + h, 1), :] = cs[s, t, pl.ds(2 * H + h, 1), :]
                ya[t, pl.ds(3 * H * X + 2 * H + s * H + h, 1), :] = row(
                    adm, depth_x(s, 0), h, depth_y(t, 2), OUT, PAD)
            ya[t, pl.ds(h * X, X), :] = flat(even)[line(even, h, depth_y(t, 0), 1, PAD), :]
            for d in range(2):
                ya[t, pl.ds(((d + 1) * H + h) * X, X), :] = flat_a[line(adm, h, depth_y(t, d), OUT, PAD), :]
        for s in range(2):
            for h in range(H):
                for d in range(2):
                    ya[t, pl.ds(h * X + depth_x(s, d), 1), :] = cs[s, t, pl.ds(d * H + h, 1), :]
        pending[0].append(both(lambda now: to_y(t, ya.at[t], yar.at[1 - t], now)))
    loaded(("o", "n"), "middle")
    for k in range(STEPS):
        done = 3 - k
        if k == STEPS - 1:
            loop(X, lambda x: alone(x, every, *states[k]), 4)
            break
        loop(X - 2 * done, lambda i: alone(i + done, every, *states[k]), (5, 6, 7)[k])
        for t in range(2):
            for h in range(H):
                dst = states[k][3]
                ys[k, t, h] = flat(dst)[line(dst, h, depth_y(t, 0), 1, PAD), :]
                for s in range(2):
                    if k < 2:
                        for d in range(2 - k):
                            ys[k, t, h, pl.ds(depth_x(s, d), 1), :] = (
                                fs[k, s, h, pl.ds(depth_y(t, 0), 1), :] if d == 0
                                else cs[s, t, pl.ds((8 + d) * H + h, 1), :])
            if k < 2:
                pending[k + 1].append(both(lambda now: to_y(t, ys.at[k, t], yr.at[k, 1 - t], now)))
            else:
                pending[k + 1].append(to_y(t, ys.at[k, t], yr.at[k, 1 - t], late | early))
        if k == 1:
            greet(early)
            for start in starts:
                start(early)

    def own_rows(k, t, h):
        return ya[t, pl.ds(h * X, X), :] if k == 0 else ys[k - 1, t, h]

    def their_rows(k, t, h):
        return yar[t, pl.ds(h * X, X), :] if k == 0 else yr[k - 1, t, h]

    def own_plane(k, s, h, at, size):
        return x0[s, pl.ds(h * Y + at, size), :] if k == 0 else fs[k - 1, s, h, pl.ds(at, size), :]

    def their_plane(k, s, h, at, size):
        return x0r[s, pl.ds(h * Y + at, size), :] if k == 0 else fr[k - 1, s, h, pl.ds(at, size), :]

    def sources(k, then, dst):
        def plane(s, d, value):
            x = depth_x(s, d) + OUT

            def part(j):
                for h in range(H):
                    add = adm[x, h, rows(j, PAD), :] * value(k, s, h, 8 * j, 8)
                    then[x, h, rows(j, WIDE), :] = then[x, h, rows(j, WIDE), :] + add
                    dst[x, h, rows(j, WIDE), :] = dst[x, h, rows(j, WIDE), :] + al * add

            loop(T, part, T)

        def lines(y, h, value):
            add = flat_a[line(adm, h, y, OUT, PAD), :] * value
            for ref, scale in ((then, 1.0), (dst, al)):
                at = line(ref, h, y, OUT, WIDE)
                flat(ref)[at, :] = flat(ref)[at, :] + scale * add

        def cell(s, t, dx, dy, h, value):
            x, y = depth_x(s, dx) + OUT, depth_y(t, dy)
            add = adm[x, h, pl.ds(PAD + y, 1), :] * value
            at = pl.ds(WIDE + y, 1)
            then[x, h, at, :] = then[x, h, at, :] + add
            dst[x, h, at, :] = dst[x, h, at, :] + al * add

        if k == 0:
            for s in range(2):
                plane(s, 0, their_plane)
                plane(s, -1, own_plane)
        for t in range(2):
            for h in range(H):
                lines(depth_y(t, 0), h, their_rows(k, t, h))
                lines(depth_y(t, -1), h, own_rows(k, t, h))
        for s, t in sides:
            base = (0, 8, 11)[k]
            for h in range(H):
                def at(i):
                    return cr[s, t, pl.ds((base + i) * H + h, 1), :]

                cell(s, t, -1, 0, h, at(0))
                cell(s, t, 0, -1, h, at(0))
                if k < 2:
                    cell(s, t, -2, 0, h, at(1))
                    cell(s, t, 0, -2, h, at(2))
                    beside = their_plane(k, s, h, depth_y(t, 0), 1)
                    if k == 0:
                        beside = beside + yar[t, pl.ds(h * X + depth_x(s, 0), 1), :]
                    else:
                        beside = beside + yr[k - 1, t, h, pl.ds(depth_x(s, 0), 1), :]
                    cell(s, t, -1, -1, h, beside)
                if k == 0:
                    cell(s, t, -3, 0, h, at(3))
                    cell(s, t, 0, -3, h, at(4))
                    cell(s, t, -2, -1, h, x0r[s, pl.ds(extra + t * H + h, 1), :])
                    cell(s, t, -1, -2, h, yar[t, pl.ds(3 * H * X + s * H + h, 1), :])

    for entry in pending[0]:
        arrived(entry)
    def place(d):
        for s in range(2):
            def part(j, s=s):
                for h in range(H):
                    adm[depth_x(s, -1 - d) + OUT, h, rows(j, PAD), :] = x0r[
                        s, rows(j, ((d + 1) * H + h) * Y + 16 * d), :]

            loop(T, part, T)

    place(0)
    for t in range(2):
        for h in range(H):
            for d in range(2):
                flat_a[line(adm, h, depth_y(t, -1 - d), OUT, PAD), :] = yar[t, pl.ds(((d + 1) * H + h) * X, X), :]
            for s in range(2):
                def put(dx, dy, value, s=s, t=t, h=h):
                    adm[depth_x(s, dx) + OUT, h, pl.ds(PAD + depth_y(t, dy), 1), :] = value

                put(0, -3, yar[t, pl.ds(3 * H * X + 2 * H + s * H + h, 1), :])
                for i, d in enumerate((-3, -2)):
                    put(d, 0, x0r[s, pl.ds(extra + 2 * H * (i + 1) + t * H + h, 1), :])
                for i, (dx, dy) in enumerate(near[:3]):
                    put(-1 - dx, -1 - dy, cr[s, t, pl.ds((5 + i) * H + h, 1), :])
    sources(0, dB, dD)

    around = [-1, 0, T - 1, T]
    full = list(range(-1, T + 1))
    frames = {
        1: [(-2, every), (-1, full), (0, full), (1, full)],
        2: [(-1, every), (0, full), (1, full), (2, full)],
        3: [(0, every), (1, every), (2, every), (3, every)],
    }
    for k in range(1, STEPS):
        now, then = (dA, dB) if k % 2 == 0 else (dB, dA)
        src, dst = (dE, dD) if k % 2 == 0 else (dD, dE)
        last_step = k == STEPS - 1

        step = (now, then, src, None if last_step else dst, k == 1)
        inner = k + 1
        middle = [0, T - 1] if last_step else around
        loop(X - 2 * inner, lambda i: coupled(i + inner, middle, *step), (0, 6, 5, 8)[k])

        def faces(s):
            for d, tiles in frames[k]:
                if d not in (0, -1):
                    coupled(end(s, d), tiles, *step)

        def touching(s):
            for d, tiles in frames[k]:
                if d == 0:
                    coupled(end(s, d), tiles, *step, lambda h, at, size: their_plane(k, s, h, at, size))
                if d == -1:
                    coupled(end(s, d), tiles, *step, lambda h, at, size: own_plane(k, s, h, at, size))

        if k == 1:
            for entry in second:
                arrived(entry)
            place(1)
        loop(2, faces)
        for entry in pending[k]:
            arrived(entry)
        loop(2, touching)
        if not last_step:
            sources(k, then, dst)

    for t in range(2):
        for h in range(H):
            at = line(A, h, depth_y(t, 0), 0, 0)
            flat(A)[at, :] = flat(A)[at, :] + (
                flat_a[line(adm, h, depth_y(t, 0), OUT, PAD), :] * yr[STEPS - 2, t, h])

    for at, (size, ok) in enumerate(in_flight):
        @pl.when(ok)
        def _():
            whole = flat(dE).at[pl.ds(0, size)]
            pltpu.make_async_copy(whole, whole, send_sem.at[at]).wait()


def store_kernel(a, b, o, n, p_out, q_out, o_out, n_out, sems):
    pairs = ((a, p_out), (b, q_out), (o, o_out), (n, n_out))
    for at, (src, dst) in enumerate(pairs):
        for h in range(2):
            pltpu.make_async_copy(src.at[:, h], dst.at[:, :, pl.ds(LANES * h, LANES)], sems.at[at]).start()
    for at, (src, dst) in enumerate(pairs):
        pltpu.make_async_copy(src, src, sems.at[at]).wait()


def per_device(nx, ny, pressure, previous, oxygen_aux, nitrogen_aux, cell_class, wall_admittance, medium):
    X, Y, Z = pressure.shape
    H = Z // LANES
    split = (X, H, Y, LANES)
    padded = (X + 2, H, Y + 2 * PAD, LANES)
    wide = (X + 2 * OUT, H, Y + 2 * WIDE, LANES)
    hbm = pl.BlockSpec(memory_space=pl.ANY)
    vmem = pl.BlockSpec(memory_space=pltpu.VMEM)
    smem = pl.BlockSpec(memory_space=pltpu.SMEM)
    f32 = jnp.float32
    rows_y = 3 * H * X + 8
    state = pl.pallas_call(
        functools.partial(steps_kernel, nx, ny),
        out_shape=[pltpu.VMEM(split, f32)] * 4,
        in_specs=[hbm] * 5 + [smem] * 2,
        out_specs=[vmem] * 4,
        scratch_shapes=[
            pltpu.VMEM(split, jnp.int32),
            pltpu.VMEM((X + 2 * OUT, H, Y + 2 * PAD, LANES), f32),
            pltpu.VMEM(padded, f32),
            pltpu.VMEM(padded, f32),
            *[pltpu.VMEM(wide, f32)] * 6,
            pltpu.VMEM((2, 3 * H * Y + 16, LANES), f32),
            pltpu.VMEM((STEPS - 1, 2, H, Y, LANES), f32),
            pltpu.VMEM((STEPS - 1, 2, H, X, LANES), f32),
            pltpu.VMEM((2, rows_y, LANES), f32),
            pltpu.VMEM((2, 2, 24, LANES), f32),
            pltpu.VMEM((2, 3 * H * Y + 16, LANES), f32),
            pltpu.VMEM((STEPS - 1, 2, H, Y, LANES), f32),
            pltpu.VMEM((STEPS - 1, 2, H, X, LANES), f32),
            pltpu.VMEM((2, rows_y, LANES), f32),
            pltpu.VMEM((2, 2, 24, LANES), f32),
            pltpu.SemaphoreType.DMA((6,)),
            pltpu.SemaphoreType.DMA((8,)),
            pltpu.SemaphoreType.DMA((26,)),
        ],
        compiler_params=pltpu.CompilerParams(
            collective_id=0, has_side_effects=True, vmem_limit_bytes=56 << 20),
    )(pressure, previous, oxygen_aux, nitrogen_aux, cell_class, wall_admittance, medium)
    out = pl.pallas_call(
        store_kernel,
        out_shape=[jax.ShapeDtypeStruct((X, Y, Z), f32)] * 4,
        in_specs=[vmem] * 4,
        out_specs=[hbm] * 4,
        scratch_shapes=[pltpu.SemaphoreType.DMA((4,))],
        compiler_params=pltpu.CompilerParams(vmem_limit_bytes=16 << 20),
    )(*state)
    return tuple(out)


def solution(mesh):
    field = P("gx", "gy", None)
    return jax.shard_map(
        functools.partial(per_device, mesh.shape["gx"], mesh.shape["gy"]),
        mesh=mesh,
        in_specs=(field,) * 5 + (P(), P()),
        out_specs=(field,) * 4,
        check_vma=False,
    )
```

time: 20.7 us -> 18.7 us (0.903)
  Pallas kernels: 20 us -> 18 us
    pallas_call x1, Pallas kernels: 17.9 us -> 16 us  [per_device(): pl.pallas_call(functools.partial(steps_kernel, nx, ny), out_shape=[pltpu....]
where the time goes in v4:
time: 18.7 us; the launch traced here: 18.6 us
  Pallas kernels  18 us (96%)
  between operations  0.64 us (3%)
    pallas_call x1, Pallas kernels, per_device(): pl.pallas_call(functools.partial(steps_kernel, nx, ny), out_shape=[pltpu....  16 us
    pallas_call x1, Pallas kernels, per_device(): pl.pallas_call(store_kernel, out_shape=[jax.ShapeDtypeStruct((X, Y, Z), f...  2.04 us

profile of v4, /device:TPU:26, one launch (start us, length us, event | category | flops | bytes accessed | tf_op | source)
XLA Modules:
  0.0 18.6 jit_solution(14791012098443972858)
XLA Ops:
  0.6 16.0 %shard_map.102 = (f32[16,2,64,128]{3,2,1,0:T(8,128)S(1)}, f32[16,2,64,128]{3,2,1,0:T(8,128)S(1)}, f32[16,2,64,128]{3,2,1,0:T(8,128)S(1)}, f32[16,2,64,128]{3,2,1,0:T(8,128)S(1)}) custom-call(f32[16,64,256]{2,1,0:T(8,128)} %p_hbm.1, f32[16,64,256]{2,1,0:T(8,128)} %q_hbm.1, f32[16,64,256]{2,1,0:T(8,128)} %o_hbm.1, f32[16,64,256]{2,1,0:T(8,128)} %n_hbm.1, ...), custom_call_target="tpu_custom_call" | custom-call | tf_op jit(solution)/shard_map/pallas_call | solution.py:570
  16.6 2.0 %shard_map.103 = (f32[16,64,256]{2,1,0:T(8,128)}, f32[16,64,256]{2,1,0:T(8,128)}, f32[16,64,256]{2,1,0:T(8,128)}, f32[16,64,256]{2,1,0:T(8,128)}) custom-call(f32[16,2,64,128]{3,2,1,0:T(8,128)S(1)} %get-tuple-element.8.a, f32[16,2,64,128]{3,2,1,0:T(8,128)S(1)} %get-tuple-element.9.b, f32[16,2,64,128]{3,2,1,0:T(8,128)S(1)} %get-tuple-element.10.o, ...), custom_call_target="tpu_custom_call" | custom-call | tf_op jit(solution)/shard_map/pallas_call | solution.py:598

commit v5 on v4

--- a/solution.py
+++ b/solution.py
@@ -90,8 +90,9 @@
             total = src[x + wx - 1, h, rows(j, wpad), :] + src[x + wx + 1, h, rows(j, wpad), :]
             total = total + (src[x + wx, h, rows(j, wpad, -1), :] + src[x + wx, h, rows(j, wpad, 1), :])
             total = total + (below[h] + above[h])
-            if across is not None and 0 <= j < T:
-                total = total + across(h, 8 * j, 8)
+            beyond = across(h, j) if across is not None else None
+            if beyond is not None:
+                total = total + beyond
             a = adm[x + OUT, h, rows(j, PAD), :]
             if fresh:
                 o, n = m1 * p, m3 * p
@@ -307,9 +308,9 @@
             admit(end(s, d), s if d < 2 else None, d + 1)
 
     loaded(("p", "q"), "ends")
-    loop(2, begin)
+    loop(2, begin, 2)
     loaded(("c",), "ends")
-    loop(2, admit_ends)
+    loop(2, admit_ends, 2)
     lines_out(0, even, 1, near)
     lines_out(5, adm, OUT, near[:3])
     for s, t in sides:
@@ -333,23 +334,28 @@
         pending[0].append(both(lambda now: to_corner(
             s, t, cs.at[s, t, pl.ds(0, 16)], cr.at[1 - s, 1 - t, pl.ds(0, 16)], now)))
     second = []
-    for part, rows_sent, entries in ((0, extra + 16, pending[0]), (extra + 16, H * Y, second)):
+    by_y = [[] for _ in range(STEPS)]
+
+    def first_out(at, count, entries):
         for s in range(2):
             entries.append(both(lambda now: to_x(
-                s, x0.at[s, pl.ds(part, rows_sent)], x0r.at[1 - s, pl.ds(part, rows_sent)], now)))
+                s, x0.at[s, pl.ds(at, count)], x0r.at[1 - s, pl.ds(at, count)], now)))
+
+    first_out(0, extra + 16, pending[0])
     loaded(("o", "n"), "ends")
     for k in range(3):
         def narrow(s, k=k):
             for d in range(3 - k):
                 alone(end(s, d), every, *states[k], fs.at[k, s] if d == 0 else None)
 
-        loop(2, narrow)
+        loop(2, narrow, 2)
         if k < 2:
             lines_out(8 + 3 * k, states[k][3], 1, near[:3 if k == 0 else 1])
         if k == 1:
             for s, t in sides:
                 pending[1].append(both(lambda now: to_corner(
                     s, t, cs.at[s, t, pl.ds(16, 8)], cr.at[1 - s, 1 - t, pl.ds(16, 8)], now)))
+            first_out(extra + 16, H * Y, second)
         for layer in ((), (0, 1), (2,))[k]:
             for s in range(2):
                 pending[layer + 1].append(both(lambda now: to_x(s, fs.at[layer, s], fr.at[layer, 1 - s], now)))
@@ -372,7 +378,7 @@
             for h in range(H):
                 for d in range(2):
                     ya[t, pl.ds(h * X + depth_x(s, d), 1), :] = cs[s, t, pl.ds(d * H + h, 1), :]
-        pending[0].append(both(lambda now: to_y(t, ya.at[t], yar.at[1 - t], now)))
+        by_y[0].append(both(lambda now: to_y(t, ya.at[t], yar.at[1 - t], now)))
     loaded(("o", "n"), "middle")
     for k in range(STEPS):
         done = 3 - k
@@ -391,25 +397,44 @@
                                 fs[k, s, h, pl.ds(depth_y(t, 0), 1), :] if d == 0
                                 else cs[s, t, pl.ds((8 + d) * H + h, 1), :])
             if k < 2:
-                pending[k + 1].append(both(lambda now: to_y(t, ys.at[k, t], yr.at[k, 1 - t], now)))
+                by_y[k + 1].append(both(lambda now: to_y(t, ys.at[k, t], yr.at[k, 1 - t], now)))
             else:
-                pending[k + 1].append(to_y(t, ys.at[k, t], yr.at[k, 1 - t], late | early))
+                by_y[k + 1].append(to_y(t, ys.at[k, t], yr.at[k, 1 - t], late | early))
         if k == 1:
             greet(early)
             for start in starts:
                 start(early)
 
-    def own_rows(k, t, h):
-        return ya[t, pl.ds(h * X, X), :] if k == 0 else ys[k - 1, t, h]
-
-    def their_rows(k, t, h):
-        return yar[t, pl.ds(h * X, X), :] if k == 0 else yr[k - 1, t, h]
-
     def own_plane(k, s, h, at, size):
         return x0[s, pl.ds(h * Y + at, size), :] if k == 0 else fs[k - 1, s, h, pl.ds(at, size), :]
 
     def their_plane(k, s, h, at, size):
         return x0r[s, pl.ds(h * Y + at, size), :] if k == 0 else fr[k - 1, s, h, pl.ds(at, size), :]
+
+    sub = lax.broadcasted_iota(jnp.int32, (8, LANES), 0)
+
+    def row_beyond(k, x, h, j):
+        at = {0: (0, False, 0), T - 1: (1, False, 7), -1: (0, True, 7), T: (1, True, 0)}.get(j)
+        if at is None:
+            return None
+        t, own, r = at
+        if k == 0:
+            value = (ya if own else yar)[t, pl.ds(h * X + x, 1), :]
+        else:
+            value = (ys if own else yr)[k - 1, t, h, pl.ds(x, 1), :]
+        return jnp.where(sub == r, jnp.broadcast_to(value, (8, LANES)), 0.0)
+
+    def beyond(k, x, s=None, d=None):
+        def value(h, j):
+            total = None
+            if d is None or d >= 0:
+                total = row_beyond(k, x, h, j)
+            if d in (0, -1) and 0 <= j < T:
+                face = (their_plane if d == 0 else own_plane)(k, s, h, 8 * j, 8)
+                total = face if total is None else total + face
+            return total
+
+        return value
 
     def sources(k, then, dst):
         def plane(s, d, value):
@@ -422,12 +447,6 @@
                     dst[x, h, rows(j, WIDE), :] = dst[x, h, rows(j, WIDE), :] + al * add
 
             loop(T, part, T)
-
-        def lines(y, h, value):
-            add = flat_a[line(adm, h, y, OUT, PAD), :] * value
-            for ref, scale in ((then, 1.0), (dst, al)):
-                at = line(ref, h, y, OUT, WIDE)
-                flat(ref)[at, :] = flat(ref)[at, :] + scale * add
 
         def cell(s, t, dx, dy, h, value):
             x, y = depth_x(s, dx) + OUT, depth_y(t, dy)
@@ -440,10 +459,6 @@
             for s in range(2):
                 plane(s, 0, their_plane)
                 plane(s, -1, own_plane)
-        for t in range(2):
-            for h in range(H):
-                lines(depth_y(t, 0), h, their_rows(k, t, h))
-                lines(depth_y(t, -1), h, own_rows(k, t, h))
         for s, t in sides:
             base = (0, 8, 11)[k]
             for h in range(H):
@@ -467,32 +482,8 @@
                     cell(s, t, -2, -1, h, x0r[s, pl.ds(extra + t * H + h, 1), :])
                     cell(s, t, -1, -2, h, yar[t, pl.ds(3 * H * X + s * H + h, 1), :])
 
-    for entry in pending[0]:
-        arrived(entry)
-    def place(d):
-        for s in range(2):
-            def part(j, s=s):
-                for h in range(H):
-                    adm[depth_x(s, -1 - d) + OUT, h, rows(j, PAD), :] = x0r[
-                        s, rows(j, ((d + 1) * H + h) * Y + 16 * d), :]
-
-            loop(T, part, T)
-
-    place(0)
-    for t in range(2):
-        for h in range(H):
-            for d in range(2):
-                flat_a[line(adm, h, depth_y(t, -1 - d), OUT, PAD), :] = yar[t, pl.ds(((d + 1) * H + h) * X, X), :]
-            for s in range(2):
-                def put(dx, dy, value, s=s, t=t, h=h):
-                    adm[depth_x(s, dx) + OUT, h, pl.ds(PAD + depth_y(t, dy), 1), :] = value
-
-                put(0, -3, yar[t, pl.ds(3 * H * X + 2 * H + s * H + h, 1), :])
-                for i, d in enumerate((-3, -2)):
-                    put(d, 0, x0r[s, pl.ds(extra + 2 * H * (i + 1) + t * H + h, 1), :])
-                for i, (dx, dy) in enumerate(near[:3]):
-                    put(-1 - dx, -1 - dy, cr[s, t, pl.ds((5 + i) * H + h, 1), :])
-    sources(0, dB, dD)
+    def put(s, t, dx, dy, h, value):
+        adm[depth_x(s, dx) + OUT, h, pl.ds(PAD + depth_y(t, dy), 1), :] = value
 
     around = [-1, 0, T - 1, T]
     full = list(range(-1, T + 1))
@@ -501,44 +492,70 @@
         2: [(-1, every), (0, full), (1, full), (2, full)],
         3: [(0, every), (1, every), (2, every), (3, every)],
     }
+    steps = [None] + [
+        ((dB, dA) if k % 2 == 1 else (dA, dB)) + ((dD, dE) if k % 2 == 1 else (dE, dD)) for k in range(1, STEPS)]
+    steps[STEPS - 1] = steps[STEPS - 1][:3] + (None,)
+
+    for entry in by_y[0]:
+        arrived(entry)
+    for t in range(2):
+        for h in range(H):
+            for d in range(2):
+                flat_a[line(adm, h, depth_y(t, -1 - d), OUT, PAD), :] = yar[t, pl.ds(((d + 1) * H + h) * X, X), :]
+            for s in range(2):
+                put(s, t, 0, -3, h, yar[t, pl.ds(3 * H * X + 2 * H + s * H + h, 1), :])
+
+    def first_rows(x):
+        for j in around:
+            for h in range(H):
+                add = adm[x + OUT, h, rows(j, PAD), :] * row_beyond(0, x, h, j)
+                dB[x + OUT, h, rows(j, WIDE), :] = add
+                dD[x + OUT, h, rows(j, WIDE), :] = al * add
+
+    loop(X, first_rows, 4)
     for k in range(1, STEPS):
-        now, then = (dA, dB) if k % 2 == 0 else (dB, dA)
-        src, dst = (dE, dD) if k % 2 == 0 else (dD, dE)
-        last_step = k == STEPS - 1
-
-        step = (now, then, src, None if last_step else dst, k == 1)
         inner = k + 1
-        middle = [0, T - 1] if last_step else around
-        loop(X - 2 * inner, lambda i: coupled(i + inner, middle, *step), (0, 6, 5, 8)[k])
-
-        def faces(s):
+        middle = around if k < STEPS - 1 else [0, T - 1]
+        for entry in by_y[k]:
+            arrived(entry)
+        loop(X - 2 * inner, lambda i: coupled(
+            i + inner, middle, *steps[k], k == 1, beyond(k, i + inner)), (0, 6, 5, 8)[k])
+
+    def place(d):
+        for s in range(2):
+            def part(j, s=s):
+                for h in range(H):
+                    adm[depth_x(s, -1 - d) + OUT, h, rows(j, PAD), :] = x0r[
+                        s, rows(j, ((d + 1) * H + h) * Y + 16 * d), :]
+
+            loop(T, part, T)
+
+    for entry in pending[0]:
+        arrived(entry)
+    place(0)
+    for s, t in sides:
+        for h in range(H):
+            for i, d in enumerate((-3, -2)):
+                put(s, t, d, 0, h, x0r[s, pl.ds(extra + 2 * H * (i + 1) + t * H + h, 1), :])
+            for i, (dx, dy) in enumerate(near[:3]):
+                put(s, t, -1 - dx, -1 - dy, h, cr[s, t, pl.ds((5 + i) * H + h, 1), :])
+    sources(0, dB, dD)
+    for k in range(1, STEPS):
+        def near_face(s, touching, k=k):
             for d, tiles in frames[k]:
-                if d not in (0, -1):
-                    coupled(end(s, d), tiles, *step)
-
-        def touching(s):
-            for d, tiles in frames[k]:
-                if d == 0:
-                    coupled(end(s, d), tiles, *step, lambda h, at, size: their_plane(k, s, h, at, size))
-                if d == -1:
-                    coupled(end(s, d), tiles, *step, lambda h, at, size: own_plane(k, s, h, at, size))
+                if (d in (0, -1)) == touching:
+                    coupled(end(s, d), tiles, *steps[k], k == 1, beyond(k, end(s, d), s, d))
 
         if k == 1:
             for entry in second:
                 arrived(entry)
             place(1)
-        loop(2, faces)
+        loop(2, lambda s: near_face(s, False), 2)
         for entry in pending[k]:
             arrived(entry)
-        loop(2, touching)
-        if not last_step:
-            sources(k, then, dst)
-
-    for t in range(2):
-        for h in range(H):
-            at = line(A, h, depth_y(t, 0), 0, 0)
-            flat(A)[at, :] = flat(A)[at, :] + (
-                flat_a[line(adm, h, depth_y(t, 0), OUT, PAD), :] * yr[STEPS - 2, t, h])
+        loop(2, lambda s: near_face(s, True), 2)
+        if k < STEPS - 1:
+            sources(k, steps[k][1], steps[k][3])
 
     for at, (size, ok) in enumerate(in_flight):
         @pl.when(ok)

time: 18.7 us -> 17.4 us (0.930)
  Pallas kernels: 18 us -> 16.6 us
    pallas_call x1, Pallas kernels: 16 us -> 14.5 us  [per_device(): pl.pallas_call(functools.partial(steps_kernel, nx, ny), out_shape=[pltpu....]
where the time goes in v5:
time: 17.4 us; the launch traced here: 17.2 us
  Pallas kernels  16.6 us (95%)
  between operations  0.64 us (4%)
    pallas_call x1, Pallas kernels, per_device(): pl.pallas_call(functools.partial(steps_kernel, nx, ny), out_shape=[pltpu....  14.5 us
    pallas_call x1, Pallas kernels, per_device(): pl.pallas_call(store_kernel, out_shape=[jax.ShapeDtypeStruct((X, Y, Z), f...  2.04 us

profile of v5, /device:TPU:26, one launch (start us, length us, event | category | flops | bytes accessed | tf_op | source)
XLA Modules:
  0.0 17.2 jit_solution(6800299183406411424)
XLA Ops:
  0.6 14.5 %shard_map.102 = (f32[16,2,64,128]{3,2,1,0:T(8,128)S(1)}, f32[16,2,64,128]{3,2,1,0:T(8,128)S(1)}, f32[16,2,64,128]{3,2,1,0:T(8,128)S(1)}, f32[16,2,64,128]{3,2,1,0:T(8,128)S(1)}) custom-call(f32[16,64,256]{2,1,0:T(8,128)} %p_hbm.1, f32[16,64,256]{2,1,0:T(8,128)} %q_hbm.1, f32[16,64,256]{2,1,0:T(8,128)} %o_hbm.1, f32[16,64,256]{2,1,0:T(8,128)} %n_hbm.1, ...), custom_call_target="tpu_custom_call" | custom-call | tf_op jit(solution)/shard_map/pallas_call | solution.py:587
  15.2 2.0 %shard_map.103 = (f32[16,64,256]{2,1,0:T(8,128)}, f32[16,64,256]{2,1,0:T(8,128)}, f32[16,64,256]{2,1,0:T(8,128)}, f32[16,64,256]{2,1,0:T(8,128)}) custom-call(f32[16,2,64,128]{3,2,1,0:T(8,128)S(1)} %get-tuple-element.8.a, f32[16,2,64,128]{3,2,1,0:T(8,128)S(1)} %get-tuple-element.9.b, f32[16,2,64,128]{3,2,1,0:T(8,128)S(1)} %get-tuple-element.10.o, ...), custom_call_target="tpu_custom_call" | custom-call | tf_op jit(solution)/shard_map/pallas_call | solution.py:615

commit v6 on v5

--- a/solution.py
+++ b/solution.py
@@ -429,7 +429,7 @@
             total = None
             if d is None or d >= 0:
                 total = row_beyond(k, x, h, j)
-            if d in (0, -1) and 0 <= j < T:
+            if d in (0, -1) and 0 <= j < T and k < STEPS - 1:
                 face = (their_plane if d == 0 else own_plane)(k, s, h, 8 * j, 8)
                 total = face if total is None else total + face
             return total
@@ -543,7 +543,7 @@
     for k in range(1, STEPS):
         def near_face(s, touching, k=k):
             for d, tiles in frames[k]:
-                if (d in (0, -1)) == touching:
+                if (d in (0, -1) and k < STEPS - 1) == touching:
                     coupled(end(s, d), tiles, *steps[k], k == 1, beyond(k, end(s, d), s, d))
 
         if k == 1:
@@ -553,9 +553,16 @@
         loop(2, lambda s: near_face(s, False), 2)
         for entry in pending[k]:
             arrived(entry)
-        loop(2, lambda s: near_face(s, True), 2)
         if k < STEPS - 1:
+            loop(2, lambda s: near_face(s, True), 2)
             sources(k, steps[k][1], steps[k][3])
+
+    for s in range(2):
+        x = depth_x(s, 0)
+        for j in range(T):
+            for h in range(H):
+                A[x, h, rows(j), :] = A[x, h, rows(j), :] + (
+                    adm[x + OUT, h, rows(j, PAD), :] * their_plane(STEPS - 1, s, h, 8 * j, 8))
 
     for at, (size, ok) in enumerate(in_flight):
         @pl.when(ok)

time: 17.4 us -> 17.4 us (level)
  no operation moved by 1% of the time
where the time goes in v6:
time: 17.4 us; the launch traced here: 17.2 us
  Pallas kernels  16.6 us (95%)
  between operations  0.64 us (4%)
    pallas_call x1, Pallas kernels, per_device(): pl.pallas_call(functools.partial(steps_kernel, nx, ny), out_shape=[pltpu....  14.6 us
    pallas_call x1, Pallas kernels, per_device(): pl.pallas_call(store_kernel, out_shape=[jax.ShapeDtypeStruct((X, Y, Z), f...  2.04 us

profile of v6, /device:TPU:26, one launch (start us, length us, event | category | flops | bytes accessed | tf_op | source)
XLA Modules:
  0.0 17.2 jit_solution(5864443665739249801)
XLA Ops:
  0.6 14.6 %shard_map.102 = (f32[16,2,64,128]{3,2,1,0:T(8,128)S(1)}, f32[16,2,64,128]{3,2,1,0:T(8,128)S(1)}, f32[16,2,64,128]{3,2,1,0:T(8,128)S(1)}, f32[16,2,64,128]{3,2,1,0:T(8,128)S(1)}) custom-call(f32[16,64,256]{2,1,0:T(8,128)} %p_hbm.1, f32[16,64,256]{2,1,0:T(8,128)} %q_hbm.1, f32[16,64,256]{2,1,0:T(8,128)} %o_hbm.1, f32[16,64,256]{2,1,0:T(8,128)} %n_hbm.1, ...), custom_call_target="tpu_custom_call" | custom-call | tf_op jit(solution)/shard_map/pallas_call | solution.py:594
  15.2 2.0 %shard_map.103 = (f32[16,64,256]{2,1,0:T(8,128)}, f32[16,64,256]{2,1,0:T(8,128)}, f32[16,64,256]{2,1,0:T(8,128)}, f32[16,64,256]{2,1,0:T(8,128)}) custom-call(f32[16,2,64,128]{3,2,1,0:T(8,128)S(1)} %get-tuple-element.8.a, f32[16,2,64,128]{3,2,1,0:T(8,128)S(1)} %get-tuple-element.9.b, f32[16,2,64,128]{3,2,1,0:T(8,128)S(1)} %get-tuple-element.10.o, ...), custom_call_target="tpu_custom_call" | custom-call | tf_op jit(solution)/shard_map/pallas_call | solution.py:622
